TPU v7x, 512 devices: a whole 4x8x8 slice. The times are simulated.
512 devices in a mesh: row: 16 (over y_lo, x), col: 8 (over z), scan: 4 (over y_hi, core).
Axes of the slice: x: 4, y: 8 (y_hi: 2, y_lo: 4; y = y_hi * 4 + y_lo), z: 8, core: 2. Of those that a mesh axis runs over, the one named last changes fastest.
Arguments:
- tokens: bfloat16 [64, 8, 2, 2, 128, 768], P(('scan', 'row'), 'col'), parts along dimension 0, may hold values from -6 to 6
- gain: float32 [768], replicated, may hold values from 0.5 to 1.5
- w_qkv: bfloat16 [768, 2304], replicated, may hold values from -2 to 2, as said below
- pattern: int32 [64, 8, 2, 2, 9], P(('scan', 'row'), 'col'), parts along dimension 0, may hold values 0 or 1
- counts: int32 [64, 8], P(('scan', 'row'), 'col'), parts along dimension 0, may hold values from 1 to 512, as said below
- region: int32 [1024], P('scan'), parts along dimension 0, may hold values from 0 to 65535, as said below
Outputs:
- attended: bfloat16 [64, 8, 2, 2, 128, 768], P(('scan', 'row'), 'col'), parts along dimension 0
There are 4 independent parts, one for each index of `scan`. A program takes and returns all parts, laid end to end along the dimension named above; an argument that names none is the same for every part. Nothing has to cross between parts.
Inputs may be any that keep to these rules, and one draw needn't show every extreme that they name: `w_qkv`: the weights have entries of magnitude at most 2. `counts`: some tile has all 512 tokens valid. `region`: the indices are distinct.
All inputs are finite; a program needn't handle non-finite values. No bound on the sum of `pattern` on one device may be relied on, other than what follows from the above.
Results may differ from a plain program's by a relative error of at most 0.004.
The roundings to bfloat16 on the way count: a program that leaves them out, or rounds other values in their place, can miss the bound.
Values may be sent and summed in bfloat16 or wider, within the bound.
A program may use at most 64 MiB of HBM per device.

v0:
```python
import jax
import jax.numpy as jnp
from jax import lax
from jax.sharding import PartitionSpec as P

HEADS = 12
HDIM = 64


def padded(shard, sides, width):
    for axis, dim in sides:
        size, length = (lax.axis_size(axis), shard.shape[dim])
        up = [(i, (i + 1) % size) for i in range(size - 1)]
        down = [(j, i) for i, j in up]
        last = lax.slice_in_dim(shard, length - width, length, axis=dim)
        initial = lax.slice_in_dim(shard, 0, width, axis=dim)
        before = lax.ppermute(last, axis, up)
        after = lax.ppermute(initial, axis, down)
        shard = jnp.concatenate([before, shard, after], axis=dim)
    return shard


def layer_norm(values, gain):
    floats = values.astype(jnp.float32)
    center = floats - jnp.mean(floats, axis=-1, keepdims=True)
    spread = jnp.mean(center * center, axis=-1, keepdims=True)
    return (center * lax.rsqrt(spread + 1e-05) * gain).astype(jnp.bfloat16)


def local(tokens, gain, w_qkv, pattern, counts, region):
    blk_rows, blk_cols, block, width = tokens.shape[2:]
    rows = blk_rows * blk_cols * block
    inputs = tokens[0, 0]
    normed = layer_norm(inputs, gain)
    qkv = jnp.dot(normed.reshape(rows, width), w_qkv, preferred_element_type=jnp.float32).astype(
        jnp.bfloat16
    )
    query = qkv[:, :width].reshape(blk_rows, blk_cols, block, width)
    keyval = qkv[:, width:].reshape(blk_rows, blk_cols, block, 2 * width)
    position = jnp.arange(rows, dtype=jnp.int32).reshape(blk_rows, blk_cols, block)
    valid = position < counts[0, 0]
    valid_marks = valid.astype(jnp.bfloat16)
    offset = (lax.axis_index("row") * lax.axis_size("col") + lax.axis_index("col")) * rows
    owned = (region[:, None] == offset + jnp.arange(rows, dtype=jnp.int32)[None, :]).astype(
        jnp.bfloat16
    )
    picked = jnp.dot(owned, qkv[:, width:], preferred_element_type=jnp.float32)
    region_kv = lax.psum(picked, ("row", "col")).astype(jnp.bfloat16)
    ext_kv, ext_marks = (
        padded(keyval, (("row", 0), ("col", 1)), 1),
        padded(valid_marks, (("row", 0), ("col", 1)), 1),
    )
    allowed = pattern[0, 0] > 0
    mark_list = []
    for drow in range(3):
        for dcol in range(3):
            near = ext_marks[drow : drow + blk_rows, dcol : dcol + blk_cols] > 0
            mark_list.append(near & allowed[:, :, 3 * drow + dcol][:, :, None])
    near_mask = jnp.concatenate(mark_list, axis=2)
    region_count = region_kv.shape[0]
    full_mask = jnp.concatenate(
        [near_mask, jnp.ones((blk_rows, blk_cols, region_count), bool)], axis=2
    )
    mask = full_mask[:, :, None, None, :]
    group_width = 2 * HDIM
    scale = HDIM ** (-0.5)

    def one_group(group):
        start = group * group_width
        q_group = lax.dynamic_slice_in_dim(query, start, group_width, 3).reshape(
            blk_rows, blk_cols, block, 2, HDIM
        )
        k_ext = lax.dynamic_slice_in_dim(ext_kv, start, group_width, 3)
        v_ext = lax.dynamic_slice_in_dim(ext_kv, width + start, group_width, 3)
        k_list = []
        v_list = []
        for drow in range(3):
            for dcol in range(3):
                k_list.append(k_ext[drow : drow + blk_rows, dcol : dcol + blk_cols])
                v_list.append(v_ext[drow : drow + blk_rows, dcol : dcol + blk_cols])
        region_k = lax.dynamic_slice_in_dim(region_kv, start, group_width, 1)
        region_v = lax.dynamic_slice_in_dim(region_kv, width + start, group_width, 1)
        spread_k = jnp.broadcast_to(
            region_k[None, None], (blk_rows, blk_cols, region_count, group_width)
        )
        spread_v = jnp.broadcast_to(
            region_v[None, None], (blk_rows, blk_cols, region_count, group_width)
        )
        all_k = jnp.concatenate(k_list + [spread_k], axis=2).reshape(
            blk_rows, blk_cols, -1, 2, HDIM
        )
        all_v = jnp.concatenate(v_list + [spread_v], axis=2).reshape(
            blk_rows, blk_cols, -1, 2, HDIM
        )
        scores = (
            jnp.einsum("abqhd,abkhd->abhqk", q_group, all_k, preferred_element_type=jnp.float32)
            * scale
        )
        masked = jnp.where(mask, scores, -1e30)
        top = jnp.max(masked, axis=-1, keepdims=True)
        weights = jnp.where(mask, jnp.exp(masked - top), 0.0)
        total = jnp.sum(weights, axis=-1, keepdims=True)
        probs = (weights / total).astype(jnp.bfloat16)
        out = jnp.einsum("abhqk,abkhd->abqhd", probs, all_v, preferred_element_type=jnp.float32)
        return out.astype(jnp.bfloat16).reshape(blk_rows, blk_cols, block, group_width)

    groups = lax.map(one_group, jnp.arange(HEADS // 2, dtype=jnp.int32))
    joined = jnp.transpose(groups, (1, 2, 3, 0, 4)).reshape(blk_rows, blk_cols, block, width)
    result = jnp.where(valid[:, :, :, None], joined, jnp.zeros_like(joined))
    return result[None, None]


def solution(mesh):
    in_specs = (
        P(("scan", "row"), "col", None, None, None, None),
        P(),
        P(),
        P(("scan", "row"), "col", None, None, None),
        P(("scan", "row"), "col"),
        P("scan"),
    )
    out_specs = P(("scan", "row"), "col", None, None, None, None)
    return jax.shard_map(local, mesh=mesh, in_specs=in_specs, out_specs=out_specs, check_vma=False)
```

profile of v0, /device:TPU:64, one launch (start us, length us, event | category | flops | bytes accessed | tf_op | source)
XLA Modules:
  0.0 1037.2 jit_solution(5514513198123027051)
XLA Ops:
  1.4 3.4 collective-permute-start.4
  9.3 2.0 convolution_convert_fusion
  13.2 2.3 copy.13
  15.5 5.4 collective-permute-start
  20.9 2.3 copy.14
  24.5 3.2 fusion.16
  27.7 738.9 %all-reduce.1 = bf16[256,1536]{1,0:T(8,128)(2,1)} all-reduce(f32[256,1536]{1,0:T(8,128)} %fusion.16), channel_id=1, replica_groups=mesh['row'=16,'col'=8,'scan'=4] {'row','col'}, use_global_device_ids=true, to_apply=%region_2.0 | all-reduce | flops 393216 | bytes 2359296 | tf_op jit(solution)/shard_map/psum | solution.py:48
  767.3 4.2 collective-permute-start.6
  772.5 2.7 slice.236
  775.2 2.1 slice.253
  777.3 2.6 copy.15
  779.8 2.3 copy.16
  782.2 7.3 collective-permute-start.7
  791.0 2.2 pad_maximum_fusion.1
  793.5 2.1 collective-permute-start.2
  795.5 4.0 collective-permute-start.3
  800.7 15.3 %collective-permute-done.2 = bf16[4,1,128,1536]{2,3,1,0:T(8,128)(2,1)S(1)} collective-permute-done((bf16[4,1,128,1536]{2,3,1,0:T(8,128)(2,1)S(1)}, bf16[4,1,128,1536]{2,3,1,0:T(8,128)(2,1)S(1)}, u32[]{:S(2)}, u32[]{:S(2)}) %collective-permute-start.2) | collective-permute-done | bytes 1572896 | tf_op jit(solution)/shard_map/ppermute | solution.py:17
  815.9 1.9 collective-permute-done.3
  817.9 4.3 pad_maximum_fusion
  822.2 210.6 %while.12 = (s32[]{:T(128)}, bf16[6,2,2,128,128]{3,4,0,2,1:T(8,128)(2,1)}, s32[6]{0:T(128)S(1)}, bf16[4,4,128,1536]{2,3,1,0:T(8,128)(2,1)}, bf16[256,1536]{0,1:T...) while((s32[]{:T(128)}, ...), condition=%wide.region_6.7_spmd, body=%wide.region_3.6_spmd.sunk | while | flops 379258240 | bytes 21140156 | solution.py:107
  827.0 1.8 dynamic-slice_dynamic-update-slice_fusion.30
  832.2 1.8 dynamic-slice_dynamic-update-slice_fusion.33
  845.7 6.6 fusion.40
  852.3 4.3 fusion.41
  862.1 1.8 dynamic-slice_dynamic-update-slice_fusion.30
  867.3 1.8 dynamic-slice_dynamic-update-slice_fusion.33
  880.8 6.6 fusion.40
  887.4 4.3 fusion.41
  897.1 1.8 dynamic-slice_dynamic-update-slice_fusion.30
  902.4 1.8 dynamic-slice_dynamic-update-slice_fusion.33
  915.9 6.6 fusion.40
  922.5 4.3 fusion.41
  932.3 1.8 dynamic-slice_dynamic-update-slice_fusion.30
  935.7 1.7 dynamic-slice_dynamic-update-slice_fusion.32
  937.5 1.8 dynamic-slice_dynamic-update-slice_fusion.33
  951.0 6.6 fusion.40
  957.6 4.3 fusion.41
  967.3 1.8 dynamic-slice_dynamic-update-slice_fusion.30
  970.8 1.7 dynamic-slice_dynamic-update-slice_fusion.32
  972.6 1.8 dynamic-slice_dynamic-update-slice_fusion.33
  986.1 6.6 fusion.40
  992.7 4.3 fusion.41
  1002.4 1.8 dynamic-slice_dynamic-update-slice_fusion.30
  1007.7 1.8 dynamic-slice_dynamic-update-slice_fusion.33
  1021.2 6.6 fusion.40
  1027.8 4.3 fusion.41
  1032.8 2.1 broadcast_select_fusion
  1034.9 2.3 copy.19
  (184 shorter events, 129.0 us)
Async XLA Ops:
  0.0 9.3 copy-start
  0.0 8.9 copy-start.3
  0.0 8.9 copy-start.4
  1.4 765.2 %collective-permute-start.4 = (bf16[1,2,128]{2,1,0:T(2,128)(2,1)}, bf16[1,2,128]{2,1,0:T(2,128)(2,1)S(1)}, u32[]{:S(2)}, u32[]{:S(2)}) collective-permute-start(bf16[1,2,128]{2,1,0:T(2,128)(2,1)} %get-tuple-element.160), channel_id=1, source_target_pairs={{0,32},{32,64},{64,96},{96,128},{128,160},{160,192},{192,224},{224... | collective-permute-start | bytes 1544 | tf_op jit(solution)/shard_map/ppermute | solution.py:17
  4.8 761.8 %collective-permute-start.5 = (bf16[1,2,128]{2,1,0:T(2,128)(2,1)}, bf16[1,2,128]{2,1,0:T(2,128)(2,1)S(1)}, u32[]{:S(2)}, u32[]{:S(2)}) collective-permute-start(bf16[1,2,128]{2,1,0:T(2,128)(2,1)} %get-tuple-element.161), channel_id=1, source_target_pairs={{32,0},{64,32},{96,64},{128,96},{160,128},{192,160},{224,192},{256... | collective-permute-start | bytes 1544 | tf_op jit(solution)/shard_map/ppermute | solution.py:18
  11.3 1.9 copy-start.2
  13.2 11.3 %copy-start.14 = (s32[256]{0:T(256)S(1)}, s32[256]{0:T(256)}, u32[]{:S(2)}) copy-start(s32[256]{0:T(256)} %param.13) | copy-start | bytes 3076
  15.5 775.5 %collective-permute-start = (bf16[1,2,128,1536]{2,3,1,0:T(8,128)(2,1)}, bf16[1,2,128,1536]{2,3,1,0:T(8,128)(2,1)}, u32[]{:S(2)}, u32[]{:S(2)}) collective-permute-start(bf16[1,2,128,1536]{2,3,1,0:T(8,128)(2,1)} %copy.13), channel_id=1, source_target_pairs={{0,32},{32,64},{64,96},{96,128},{128,160},{160,192},{192,224},{224... | collective-permute-start | bytes 2359304 | tf_op jit(solution)/shard_map/ppermute | solution.py:17
  23.2 767.8 %collective-permute-start.1 = (bf16[1,2,128,1536]{2,3,1,0:T(8,128)(2,1)}, bf16[1,2,128,1536]{2,3,1,0:T(8,128)(2,1)}, u32[]{:S(2)}, u32[]{:S(2)}) collective-permute-start(bf16[1,2,128,1536]{2,3,1,0:T(8,128)(2,1)} %copy.14), channel_id=1, source_target_pairs={{32,0},{64,32},{96,64},{128,96},{160,128},{192,160},{224,192},{256... | collective-permute-start | bytes 2359304 | tf_op jit(solution)/shard_map/ppermute | solution.py:18
  27.7 738.9 %copy-start.13 = (s32[1,1,2,2,9]{4,3,2,1,0:T(2,128)S(1)}, s32[1,1,2,2,9]{4,3,2,1,0:T(2,128)}, u32[]{:S(2)}) copy-start(s32[1,1,2,2,9]{4,3,2,1,0:T(2,128)} %param.11) | copy-start | bytes 436
  767.3 22.2 %collective-permute-start.6 = (bf16[4,1,128]{2,1,0:T(2,128)(2,1)}, bf16[4,1,128]{2,1,0:T(2,128)(2,1)S(1)}, u32[]{:S(2)}, u32[]{:S(2)}) collective-permute-start(bf16[4,1,128]{2,1,0:T(2,128)(2,1)} %get-tuple-element.159), channel_id=1, source_target_pairs={{0,4},{4,8},{8,12},{12,16},{16,20},{20,24},{24,28},{1,5},{5,9},{9,... | collective-permute-start | bytes 3080 | tf_op jit(solution)/shard_map/ppermute | solution.py:17
  782.2 17.4 %collective-permute-start.7 = (bf16[4,1,128]{2,1,0:T(2,128)(2,1)}, bf16[4,1,128]{2,1,0:T(2,128)(2,1)S(1)}, u32[]{:S(2)}, u32[]{:S(2)}) collective-permute-start(bf16[4,1,128]{2,1,0:T(2,128)(2,1)} %get-tuple-element.158), channel_id=1, source_target_pairs={{4,0},{8,4},{12,8},{16,12},{20,16},{24,20},{28,24},{5,1},{9,5},{13... | collective-permute-start | bytes 3080 | tf_op jit(solution)/shard_map/ppermute | solution.py:18
  793.2 6.4 copy-start.12
  793.2 6.5 copy-start.11
  793.2 6.5 copy-start.7
  793.2 7.1 copy-start.10
  793.2 7.2 copy-start.9
  793.2 7.2 copy-start.6
  793.3 7.3 copy-start.8
  793.3 24.6 %copy-start.1 = (bf16[2,2,128,1536]{2,3,1,0:T(8,128)(2,1)S(1)}, bf16[2,2,128,1536]{2,3,1,0:T(8,128)(2,1)}, u32[]{:S(2)}) copy-start(bf16[2,2,128,1536]{2,3,1,0:T(8,128)(2,1)} %copy.15) | copy-start | bytes 4718596
  793.5 22.4 %collective-permute-start.2 = (bf16[4,1,128,1536]{2,3,1,0:T(8,128)(2,1)S(1)}, bf16[4,1,128,1536]{2,3,1,0:T(8,128)(2,1)S(1)}, u32[]{:S(2)}, u32[]{:S(2)}) collective-permute-start(bf16[4,1,128,1536]{2,3,1,0:T(8,128)(2,1)S(1)} %get-tuple-element.154), channel_id=1, source_target_pairs={{0,4},{4,8},{8,12},{12,16},{16,20},{20,24},{24,28},{1,5},{5,9},{9,... | collective-permute-start | bytes 4718600 | tf_op jit(solution)/shard_map/ppermute | solution.py:17
  795.5 22.3 %collective-permute-start.3 = (bf16[4,1,128,1536]{2,3,1,0:T(8,128)(2,1)S(1)}, bf16[4,1,128,1536]{2,3,1,0:T(8,128)(2,1)S(1)}, u32[]{:S(2)}, u32[]{:S(2)}) collective-permute-start(bf16[4,1,128,1536]{2,3,1,0:T(8,128)(2,1)S(1)} %get-tuple-element.155), channel_id=1, source_target_pairs={{4,0},{8,4},{12,8},{16,12},{20,16},{24,20},{28,24},{5,1},{9,5},{13... | collective-permute-start | bytes 4718600 | tf_op jit(solution)/shard_map/ppermute | solution.py:18
  800.7 21.5 %copy-start.15 = (pred[2,2,1408]{2,1,0:T(4,128)(4,1)}, pred[2,2,1408]{2,1,0:T(4,128)(4,1)S(1)}, u32[]{:S(2)}) copy-start(pred[2,2,1408]{2,1,0:T(4,128)(4,1)S(1)} %constant_dynamic-update-slice_fusion.1) | copy-start | bytes 16900
  822.2 210.6 %copy-start.5 = (pred[2,2,128]{2,1,0:T(4,128)(4,1)S(1)}, pred[2,2,128]{2,1,0:T(4,128)(4,1)}, u32[]{:S(2)}) copy-start(pred[2,2,128]{2,1,0:T(4,128)(4,1)} %get-tuple-element.163) | copy-start | bytes 1540
  822.2 11.7 %copy-start.17 = (s32[6]{0:T(128)}, s32[6]{0:T(128)S(1)}, u32[]{:S(2)}) copy-start(s32[6]{0:T(128)S(1)} %get-tuple-element.283) | copy-start | bytes 76 | tf_op jit(solution)/shard_map/while
  834.0 11.8 %copy-start.16 = (pred[2,2,1,1,1408]{4,1,0,3,2:T(4,128)(4,1)S(1)}, pred[2,2,1,1,1408]{4,1,0,3,2:T(4,128)(4,1)}, u32[]{:S(2)}) copy-start(pred[2,2,1,1,1408]{4,1,0,3,2:T(4,128)(4,1)} %get-tuple-element.286) | copy-start | bytes 16900 | tf_op jit(solution)/shard_map/while
  852.3 5.0 copy-start.18
  857.3 11.7 %copy-start.17 = (s32[6]{0:T(128)}, s32[6]{0:T(128)S(1)}, u32[]{:S(2)}) copy-start(s32[6]{0:T(128)S(1)} %get-tuple-element.283) | copy-start | bytes 76 | tf_op jit(solution)/shard_map/while
  869.0 11.8 %copy-start.16 = (pred[2,2,1,1,1408]{4,1,0,3,2:T(4,128)(4,1)S(1)}, pred[2,2,1,1,1408]{4,1,0,3,2:T(4,128)(4,1)}, u32[]{:S(2)}) copy-start(pred[2,2,1,1,1408]{4,1,0,3,2:T(4,128)(4,1)} %get-tuple-element.286) | copy-start | bytes 16900 | tf_op jit(solution)/shard_map/while
  887.4 5.0 copy-start.18
  892.4 11.7 %copy-start.17 = (s32[6]{0:T(128)}, s32[6]{0:T(128)S(1)}, u32[]{:S(2)}) copy-start(s32[6]{0:T(128)S(1)} %get-tuple-element.283) | copy-start | bytes 76 | tf_op jit(solution)/shard_map/while
  904.1 11.8 %copy-start.16 = (pred[2,2,1,1,1408]{4,1,0,3,2:T(4,128)(4,1)S(1)}, pred[2,2,1,1,1408]{4,1,0,3,2:T(4,128)(4,1)}, u32[]{:S(2)}) copy-start(pred[2,2,1,1,1408]{4,1,0,3,2:T(4,128)(4,1)} %get-tuple-element.286) | copy-start | bytes 16900 | tf_op jit(solution)/shard_map/while
  922.5 5.0 copy-start.18
  927.5 11.7 %copy-start.17 = (s32[6]{0:T(128)}, s32[6]{0:T(128)S(1)}, u32[]{:S(2)}) copy-start(s32[6]{0:T(128)S(1)} %get-tuple-element.283) | copy-start | bytes 76 | tf_op jit(solution)/shard_map/while
  939.2 11.8 %copy-start.16 = (pred[2,2,1,1,1408]{4,1,0,3,2:T(4,128)(4,1)S(1)}, pred[2,2,1,1,1408]{4,1,0,3,2:T(4,128)(4,1)}, u32[]{:S(2)}) copy-start(pred[2,2,1,1,1408]{4,1,0,3,2:T(4,128)(4,1)} %get-tuple-element.286) | copy-start | bytes 16900 | tf_op jit(solution)/shard_map/while
  957.6 5.0 copy-start.18
  962.6 11.7 %copy-start.17 = (s32[6]{0:T(128)}, s32[6]{0:T(128)S(1)}, u32[]{:S(2)}) copy-start(s32[6]{0:T(128)S(1)} %get-tuple-element.283) | copy-start | bytes 76 | tf_op jit(solution)/shard_map/while
  974.3 11.8 %copy-start.16 = (pred[2,2,1,1,1408]{4,1,0,3,2:T(4,128)(4,1)S(1)}, pred[2,2,1,1,1408]{4,1,0,3,2:T(4,128)(4,1)}, u32[]{:S(2)}) copy-start(pred[2,2,1,1,1408]{4,1,0,3,2:T(4,128)(4,1)} %get-tuple-element.286) | copy-start | bytes 16900 | tf_op jit(solution)/shard_map/while
  992.7 5.0 copy-start.18
  997.7 11.7 %copy-start.17 = (s32[6]{0:T(128)}, s32[6]{0:T(128)S(1)}, u32[]{:S(2)}) copy-start(s32[6]{0:T(128)S(1)} %get-tuple-element.283) | copy-start | bytes 76 | tf_op jit(solution)/shard_map/while
  1009.4 11.8 %copy-start.16 = (pred[2,2,1,1,1408]{4,1,0,3,2:T(4,128)(4,1)S(1)}, pred[2,2,1,1,1408]{4,1,0,3,2:T(4,128)(4,1)}, u32[]{:S(2)}) copy-start(pred[2,2,1,1,1408]{4,1,0,3,2:T(4,128)(4,1)} %get-tuple-element.286) | copy-start | bytes 16900 | tf_op jit(solution)/shard_map/while
  1027.8 5.0 copy-start.18
where the time goes:
time: 1040 us
  blocking collectives  739 us (71%)
  local copies, waits for them, and re-layouts  162 us (16%)
  matrix products  70.5 us (7%)
  starting transfers between devices  28.9 us (3%)
  waiting for transfers between devices  17.2 us (2%)
  other arithmetic  14.3 us (1%)
    psum x1, blocking collectives, local(): region_kv = lax.psum(picked, ('row', 'col')).astype(jnp.bfloat16)  739 us
    while x96, local copies, waits for them, and re-layouts  103 us
    sub x6, matrix products, one_group(): weights = jnp.where(mask, jnp.exp(masked - top), 0.0)  39.5 us
    dot_general x6, matrix products, one_group(): jnp.einsum('abhqk,abkhd->abqhd', probs, all_v, preferred_element_type=jnp...  25.8 us
  transfers between devices with their start and end apart: 8, of which 2 were waited for; matrix products, arithmetic and copies ran while one was open for 3% of the time, Pallas kernels for 0%

commit v1 on v0

v1 whole, which is shorter than its diff:
```python
import functools

import jax
import jax.numpy as jnp
from jax import lax
from jax.experimental import pallas as pl
from jax.experimental.pallas import tpu as pltpu
from jax.sharding import PartitionSpec as P

HEADS = 12
HDIM = 64
BLK = 128
WIDTH = HEADS * HDIM
AUG = 2 * HDIM
REGION = 256
MESH = pl.DeviceIdType.MESH
EXP_SCALE = (HDIM ** (-0.5)) * 1.4426950408889634
FAR = -1e30
LOW, HIGH = 2.0 ** (-80), 2.0**100

SLOTS = ((0, 1), (0, 2), (3, 1), (3, 2), (1, 0), (2, 0), (1, 3), (2, 3), (0, 0), (0, 3), (3, 0), (3, 3))
OWN = ((1, 1), (1, 2), (2, 1), (2, 2))
OWN_KEYS = 4 * BLK
HALO_KEYS = len(SLOTS) * BLK
REGION_AT = OWN_KEYS + HALO_KEYS
KEYS = REGION_AT + REGION


def dot(a, b):
    return lax.dot_general(a, b, (((1,), (0,)), ((), ())), preferred_element_type=jnp.float32)


def dot_t(a, b):
    return lax.dot_general(a, b, (((1,), (1,)), ((), ())), preferred_element_type=jnp.float32)


def norm_rows(values, gain):
    floats = values.astype(jnp.float32)
    center = floats - jnp.sum(floats, axis=-1, keepdims=True) * (1.0 / WIDTH)
    spread = jnp.sum(center * center, axis=-1, keepdims=True) * (1.0 / WIDTH)
    return (center * lax.rsqrt(spread + 1e-05) * gain).astype(jnp.bfloat16)


def tile_of(place):
    return tuple((0, 1, 1, 2)[p] for p in place), tuple((1, 0, 1, 0)[p] for p in place)


def kernel(
    n_row, n_col,
    tok_hbm, gain_ref, w_hbm, pat_ref, cnt_ref, reg_ref,
    out_ref, flag_ref, halo_out, rtok_out, cnts_out,
    own, halo, weights, cnts, picks, part1, mine, part2, rtok, normed, qa, ka, va, oa,
    load_sem, halo_send, halo_recv, cnt_send, cnt_recv, p1_send, p1_recv, p2_send, p2_recv, p3_send, p3_recv, save_sem,
):
    row, col = lax.axis_index("row"), lax.axis_index("col")
    up, down, left, right = row > 0, row < n_row - 1, col > 0, col < n_col - 1
    exists_r, exists_c = (up, None, None, down), (left, None, None, right)
    chunk = REGION // n_row

    def both(a, b):
        return b if a is None else (a if b is None else a & b)

    def there(place):
        return both(exists_r[place[0]], exists_c[place[1]])

    loads = [
        pltpu.make_async_copy(tok_hbm, own, load_sem.at[0]),
        pltpu.make_async_copy(w_hbm, weights, load_sem.at[1]),
    ]
    for load in loads:
        load.start()

    barrier = pltpu.get_barrier_semaphore()
    diagonals = [(dr, dc) for dr in (-1, 1) for dc in (-1, 1)]

    def signal_row(r, _):
        @pl.when(r != row)
        def _():
            pl.semaphore_signal(barrier, inc=1, device_id={"row": r}, device_id_type=MESH)
        return 0

    def signal_col(c, _):
        @pl.when(c != col)
        def _():
            pl.semaphore_signal(barrier, inc=1, device_id={"col": c}, device_id_type=MESH)
        return 0

    lax.fori_loop(0, n_row, signal_row, 0)
    lax.fori_loop(0, n_col, signal_col, 0)
    for dr, dc in diagonals:
        @pl.when(both(up if dr < 0 else down, left if dc < 0 else right))
        def _(dr=dr, dc=dc):
            pl.semaphore_signal(barrier, inc=1, device_id={"row": row + dr, "col": col + dc}, device_id_type=MESH)

    as_int = lambda flag: jnp.where(flag, 1, 0)
    n_diag = (as_int(up) + as_int(down)) * (as_int(left) + as_int(right))

    for group in range(4):
        @pl.when(jnp.logical_not((up, down, left, right)[group]))
        def _(group=group):
            halo[2 * group : 2 * group + 2] = jnp.zeros((2, BLK, WIDTH), jnp.bfloat16)
    for slot in range(8, 12):
        @pl.when(jnp.logical_not(there(SLOTS[slot])))
        def _(slot=slot):
            halo[slot] = jnp.zeros((BLK, WIDTH), jnp.bfloat16)
    count = cnt_ref[0, 0]
    for t in range(9):
        if t == 4:
            cnts[t] = jnp.broadcast_to(count, (8, 128)).astype(jnp.int32)
        else:
            dr, dc = t // 3 - 1, t % 3 - 1
            exists = both((up, None, down)[dr + 1], (left, None, right)[dc + 1])

            @pl.when(jnp.logical_not(exists))
            def _(t=t):
                cnts[t] = jnp.zeros((8, 128), jnp.int32)

    loads[0].wait()
    pl.semaphore_wait(barrier, n_row + n_col - 2 + n_diag)

    def remote(src, dst, send, recv, device):
        return pltpu.make_async_remote_copy(
            src_ref=src, dst_ref=dst, send_sem=send, recv_sem=recv, device_id=device, device_id_type=MESH
        )

    sends = []

    def send_halo(cond, src, slot, device):
        copy = remote(src, halo.at[slot], halo_send.at[len(sends)], halo_recv.at[slot], device)
        sends.append((cond, copy))
        pl.when(cond)(lambda: copy.start())

    def halo_wait(slots):
        for slot in slots:
            copy = remote(halo.at[slot], halo.at[slot], halo_send.at[slot], halo_recv.at[slot], {"row": row})
            pl.when(there(SLOTS[slot]))(lambda copy=copy: copy.wait_recv())

    send_halo(up, own.at[0], 2, {"row": row - 1})
    send_halo(up, own.at[1], 3, {"row": row - 1})
    send_halo(down, own.at[2], 0, {"row": row + 1})
    send_halo(down, own.at[3], 1, {"row": row + 1})

    cnt_copies = []
    for t in range(9):
        if t != 4:
            dr, dc = t // 3 - 1, t % 3 - 1
            exists = both((up, None, down)[dr + 1], (left, None, right)[dc + 1])
            device = {}
            if dr:
                device["row"] = row + dr
            if dc:
                device["col"] = col + dc
            copy = remote(cnts.at[4], cnts.at[8 - t], cnt_send.at[t], cnt_recv.at[8 - t], device)
            arrives = remote(cnts.at[4], cnts.at[t], cnt_send.at[t], cnt_recv.at[t], device)
            cnt_copies.append((exists, copy, arrives))
            pl.when(exists)(lambda copy=copy: copy.start())

    tokens = own[...].reshape(OWN_KEYS, WIDTH)
    first = (row * n_col + col) * OWN_KEYS
    flat = lax.broadcasted_iota(jnp.int32, (OWN_KEYS, REGION), 0) + first
    hit = jnp.where(flat == reg_ref[...], 1.0, 0.0).astype(jnp.bfloat16)
    found = lax.dot_general(hit, tokens, (((0,), (0,)), ((), ())), preferred_element_type=jnp.float32)
    picks[...] = found.astype(jnp.bfloat16).reshape(n_row, chunk, WIDTH)

    def exchange(size, axis, me, source, target, send_sem, recv_sem):
        def copy_to(k):
            return remote(source(k), target(me), send_sem.at[k], recv_sem.at[me], {axis: k})

        def copy_from(k):
            return remote(source(k), target(k), send_sem.at[k], recv_sem.at[k], {axis: k})

        def start(k, _):
            pl.when(k != me)(lambda: copy_to(k).start())
            return 0

        def arrive(k, _):
            pl.when(k != me)(lambda: copy_from(k).wait_recv())
            return 0

        def leave(k, _):
            pl.when(k != me)(lambda: copy_to(k).wait_send())
            return 0

        return tuple(lambda body=body: lax.fori_loop(0, size, body, 0) for body in (start, arrive, leave))

    start1, arrive1, leave1 = exchange(
        n_row, "row", row, lambda k: picks.at[k], lambda k: part1.at[k], p1_send, p1_recv
    )
    start2, arrive2, leave2 = exchange(n_col, "col", col, lambda k: mine, lambda k: part2.at[k], p2_send, p2_recv)
    start3, arrive3, leave3 = exchange(
        n_row, "row", row, lambda k: rtok.at[row], lambda k: rtok.at[k], p3_send, p3_recv
    )
    start1()
    part1[row] = picks[row]

    send_halo(left, own.at[0], 6, {"col": col - 1})
    send_halo(left, own.at[2], 7, {"col": col - 1})
    send_halo(right, own.at[1], 4, {"col": col + 1})
    send_halo(right, own.at[3], 5, {"col": col + 1})

    lane = lax.broadcasted_iota(jnp.int32, (1, AUG), 1)
    spare = lax.rem(lane, HDIM)
    low_half = lane < HDIM

    def query_marks(block):
        i, j = divmod(block, 2)
        marks = jnp.where(spare == 16, FAR, 0.0)
        for k in range(9):
            place = (i + k // 3, j + k % 3)
            allowed = pat_ref[block, k].astype(jnp.float32)
            exists = there(place)
            if exists is not None:
                allowed = allowed * as_int(exists).astype(jnp.float32)
            marks = jnp.where(spare == place[0] * 4 + place[1], (1.0 - allowed) * FAR, marks)
        return marks

    def key_marks(place):
        (tr, tc), (i, j) = tile_of(place)
        position = lax.broadcasted_iota(jnp.int32, (BLK, AUG), 0) + (i * 2 + j) * BLK
        beyond = jnp.where(position >= cnts[3 * tr + tc, 0:1, :], 1.0, 0.0)
        return jnp.where(spare == 16, beyond, jnp.where(spare == place[0] * 4 + place[1], 1.0, 0.0))

    def halves(pair, other):
        return jnp.where(low_half, pair, other), jnp.where(low_half, other, pair)

    def project(rows, key_at, marks, part, out):
        n = rows

        def body(j, _):
            at = pl.multiple_of(part * WIDTH + j * 256, 128)
            result = dot(normed[0:n, :], weights[:, pl.ds(at, 256)]).astype(jnp.bfloat16)
            for t in range(2):
                pair = result[:, t * 128 : t * 128 + 128]
                first_head, second_head = halves(pair, marks)
                to = pl.multiple_of(j * 512 + t * 256, 128)
                out[pl.ds(key_at, n), pl.ds(to, 128)] = first_head
                out[pl.ds(key_at, n), pl.ds(pl.multiple_of(to + 128, 128), 128)] = second_head
            return 0

        lax.fori_loop(0, 3, body, 0)

    def keys_values(values, key_at, places):
        n = values.shape[0]
        normed[0:n, :] = norm_rows(values, gain_ref[...])
        if places is None:
            marks = jnp.zeros((n, AUG), jnp.bfloat16)
        else:
            marks = jnp.concatenate([key_marks(place) for place in places], axis=0).astype(jnp.bfloat16)
        project(n, key_at, marks, 1, ka)
        project(n, key_at, jnp.ones((n, AUG), jnp.bfloat16), 2, va)

    def attend(blocks, key_at, n, initial=False):
        def body(h, _):
            at = pl.ds(pl.multiple_of(h * AUG, 128), AUG)
            if len(blocks) == 4:
                q = qa[:, at]
            else:
                q = jnp.concatenate([qa[pl.ds(b * BLK, BLK), at] for b in blocks], axis=0)
            scores = dot_t(q, ka[pl.ds(key_at, n), at])
            probs = jnp.exp2(scores * EXP_SCALE).astype(jnp.bfloat16)
            result = dot(probs, va[pl.ds(key_at, n), at])
            if initial:
                oa[:, at] = result
            else:
                for s, b in enumerate(blocks):
                    oa[pl.ds(b * BLK, BLK), at] += result[s * BLK : s * BLK + BLK]
            return 0

        lax.fori_loop(0, HEADS, body, 0)

    loads[1].wait()
    keys_values(tokens, 0, OWN)
    q_marks = jnp.concatenate([jnp.broadcast_to(query_marks(b), (BLK, AUG)) for b in range(4)], axis=0)
    project(OWN_KEYS, 0, q_marks.astype(jnp.bfloat16), 0, qa)

    arrive1()
    total = part1[0].astype(jnp.float32)
    for k in range(1, n_row):
        total = total + part1[k].astype(jnp.float32)
    mine[...] = total.astype(jnp.bfloat16)
    start2()
    part2[col] = mine[...]

    halo_wait((0, 1, 2, 3))
    send_halo(both(up, left), halo.at[0], 9, {"col": col - 1})
    send_halo(both(up, right), halo.at[1], 8, {"col": col + 1})
    send_halo(both(down, left), halo.at[2], 11, {"col": col - 1})
    send_halo(both(down, right), halo.at[3], 10, {"col": col + 1})

    attend((0, 1, 2, 3), 0, OWN_KEYS, initial=True)

    arrive2()
    total = part2[0].astype(jnp.float32)
    for k in range(1, n_col):
        total = total + part2[k].astype(jnp.float32)
    rtok[row] = total.astype(jnp.bfloat16)
    start3()

    for exists, _, arrives in cnt_copies:
        pl.when(exists)(lambda arrives=arrives: arrives.wait_recv())

    for group, blocks in enumerate(((0, 1), (2, 3), (0, 2), (1, 3))):
        slots = (2 * group, 2 * group + 1)
        if group >= 2:
            halo_wait(slots)
        key_at = OWN_KEYS + 2 * group * BLK
        keys_values(halo[2 * group : 2 * group + 2].reshape(2 * BLK, WIDTH), key_at, [SLOTS[s] for s in slots])
        attend(blocks, key_at, 2 * BLK)

    arrive3()
    keys_values(rtok[...].reshape(REGION, WIDTH), REGION_AT, None)
    attend((0, 1, 2, 3), REGION_AT, REGION)

    halo_wait((8, 9, 10, 11))
    saves = [
        pltpu.make_async_copy(halo, halo_out, save_sem.at[0]),
        pltpu.make_async_copy(rtok, rtok_out, save_sem.at[1]),
        pltpu.make_async_copy(cnts, cnts_out, save_sem.at[2]),
    ]
    for save in saves:
        save.start()
    keys_values(halo[8:12].reshape(4 * BLK, WIDTH), OWN_KEYS + 8 * BLK, SLOTS[8:12])
    for b in range(4):
        attend((b,), OWN_KEYS + (8 + b) * BLK, BLK)

    valid = lax.broadcasted_iota(jnp.int32, (OWN_KEYS, AUG), 0) < count

    def finish(p, bad):
        one = oa[:, pl.ds(pl.multiple_of(p * 256, 128), 128)]
        two = oa[:, pl.ds(pl.multiple_of(p * 256 + 128, 128), 128)]
        sums = pltpu.roll(jnp.where(low_half, two, one), HDIM, 1)
        result = jnp.where(low_half, one, two) / sums
        out_ref[:, pl.ds(pl.multiple_of(p * 128, 128), 128)] = jnp.where(valid, result, 0.0).astype(jnp.bfloat16)
        fine = (sums >= LOW) & (sums <= HIGH)
        return jnp.maximum(bad, jnp.max(jnp.where(fine, 0.0, 1.0), axis=0, keepdims=True))

    bad = lax.fori_loop(0, 6, finish, jnp.zeros((1, AUG), jnp.float32))
    flag_ref[...] = jnp.broadcast_to(bad, (8, AUG))

    for cond, copy in sends:
        pl.when(cond)(lambda copy=copy: copy.wait_send())
    for exists, copy, _ in cnt_copies:
        pl.when(exists)(lambda copy=copy: copy.wait_send())
    leave1()
    leave2()
    leave3()
    for save in saves:
        save.wait()


def fused(n_row, n_col, tokens, gain, w_qkv, pattern, counts, region):
    chunk = REGION // n_row
    vmem = pl.BlockSpec(memory_space=pltpu.VMEM)
    smem = pl.BlockSpec(memory_space=pltpu.SMEM)
    anywhere = pl.BlockSpec(memory_space=pl.ANY)
    bf16, f32 = jnp.bfloat16, jnp.float32
    dma = pltpu.SemaphoreType.DMA
    flops = 2 * (OWN_KEYS * WIDTH * WIDTH * 3 + (KEYS - OWN_KEYS) * WIDTH * WIDTH * 2 + OWN_KEYS * 1408 * WIDTH * 2)
    return pl.pallas_call(
        functools.partial(kernel, n_row, n_col),
        out_shape=(
            jax.ShapeDtypeStruct((OWN_KEYS, WIDTH), bf16),
            jax.ShapeDtypeStruct((8, AUG), f32),
            jax.ShapeDtypeStruct((len(SLOTS), BLK, WIDTH), bf16),
            jax.ShapeDtypeStruct((n_row, chunk, WIDTH), bf16),
            jax.ShapeDtypeStruct((9, 8, 128), jnp.int32),
        ),
        in_specs=[anywhere, vmem, anywhere, smem, smem, vmem],
        out_specs=(vmem, vmem, anywhere, anywhere, anywhere),
        scratch_shapes=[
            pltpu.VMEM((4, BLK, WIDTH), bf16),
            pltpu.VMEM((len(SLOTS), BLK, WIDTH), bf16),
            pltpu.VMEM((WIDTH, 3 * WIDTH), bf16),
            pltpu.VMEM((9, 8, 128), jnp.int32),
            pltpu.VMEM((n_row, chunk, WIDTH), bf16),
            pltpu.VMEM((n_row, chunk, WIDTH), bf16),
            pltpu.VMEM((chunk, WIDTH), bf16),
            pltpu.VMEM((n_col, chunk, WIDTH), bf16),
            pltpu.VMEM((n_row, chunk, WIDTH), bf16),
            pltpu.VMEM((OWN_KEYS, WIDTH), bf16),
            pltpu.VMEM((OWN_KEYS, HEADS * AUG), bf16),
            pltpu.VMEM((KEYS, HEADS * AUG), bf16),
            pltpu.VMEM((KEYS, HEADS * AUG), bf16),
            pltpu.VMEM((OWN_KEYS, HEADS * AUG), f32),
            dma((2,)),
            dma((12,)), dma((12,)),
            dma((9,)), dma((9,)),
            dma((n_row,)), dma((n_row,)),
            dma((n_col,)), dma((n_col,)),
            dma((n_row,)), dma((n_row,)),
            dma((3,)),
        ],
        compiler_params=pltpu.CompilerParams(
            collective_id=0, has_side_effects=True, vmem_limit_bytes=48 << 20
        ),
        cost_estimate=pl.CostEstimate(flops=flops, bytes_accessed=9 << 20, transcendentals=OWN_KEYS * 1408 * HEADS),
    )(tokens, gain, w_qkv, pattern, counts, region)


def stable(own, gain, w_qkv, pattern, row, col, n_row, n_col, halo, rtok, cnts):
    grid = {place: own[i] for i, place in enumerate(OWN)}
    grid.update({place: halo[i] for i, place in enumerate(SLOTS)})
    places = [(r, c) for r in range(4) for c in range(4)]
    rows = jnp.concatenate([grid[p] for p in places] + [rtok.reshape(REGION, WIDTH)], axis=0)
    qkv = dot(norm_rows(rows, gain), w_qkv).astype(jnp.bfloat16)
    valid = []
    for place in places:
        (tr, tc), (i, j) = tile_of(place)
        valid.append(jnp.arange(BLK) + (i * 2 + j) * BLK < cnts[3 * tr + tc, 0, 0])
    masks = []
    for block in range(4):
        i, j = divmod(block, 2)
        marks = []
        for number, (r, c) in enumerate(places):
            dr, dc = r - i, c - j
            if 0 <= dr < 3 and 0 <= dc < 3:
                a, b = row * 2 + r - 1, col * 2 + c - 1
                inside = (a >= 0) & (a < 2 * n_row) & (b >= 0) & (b < 2 * n_col)
                marks.append(valid[number] & inside & (pattern[block, 3 * dr + dc] > 0))
            else:
                marks.append(jnp.zeros((BLK,), bool))
        masks.append(jnp.concatenate(marks + [jnp.ones((REGION,), bool)]))
    mask = jnp.stack(masks)
    own_at = jnp.array([4 * r + c for r, c in OWN])
    query = qkv[: 16 * BLK, :WIDTH].reshape(16, BLK, HEADS, HDIM)[own_at]
    key = qkv[:, WIDTH : 2 * WIDTH].reshape(-1, HEADS, HDIM)
    value = qkv[:, 2 * WIDTH :].reshape(-1, HEADS, HDIM)

    def one_head(args):
        q, k, v = args
        scores = jnp.einsum("bqd,kd->bqk", q, k, preferred_element_type=jnp.float32) * (HDIM ** (-0.5))
        masked = jnp.where(mask[:, None, :], scores, -1e30)
        top = jnp.max(masked, axis=-1, keepdims=True)
        weights = jnp.where(mask[:, None, :], jnp.exp(masked - top), 0.0)
        probs = (weights / jnp.sum(weights, axis=-1, keepdims=True)).astype(jnp.bfloat16)
        return jnp.einsum("bqk,kd->bqd", probs, v, preferred_element_type=jnp.float32).astype(jnp.bfloat16)

    heads = lax.map(one_head, (query.transpose(2, 0, 1, 3), key.transpose(1, 0, 2), value.transpose(1, 0, 2)))
    joined = heads.transpose(1, 2, 0, 3).reshape(OWN_KEYS, WIDTH)
    live = jnp.arange(OWN_KEYS) < cnts[4, 0, 0]
    return jnp.where(live[:, None], joined, jnp.zeros_like(joined))


def local(n_row, n_col, tokens, gain, w_qkv, pattern, counts, region):
    own = tokens.reshape(4, BLK, WIDTH)
    blocks = pattern.reshape(4, 9)
    scale = gain.reshape(1, WIDTH)
    out, flag, halo, rtok, cnts = fused(
        n_row, n_col, own, scale, w_qkv, blocks, counts, region.reshape(1, REGION)
    )
    row, col = lax.axis_index("row"), lax.axis_index("col")
    result = lax.cond(
        jnp.max(flag) > 0.0,
        lambda: stable(own, scale, w_qkv, blocks, row, col, n_row, n_col, halo, rtok, cnts),
        lambda: out,
    )
    return result.reshape(tokens.shape)


def solution(mesh):
    in_specs = (
        P(("scan", "row"), "col", None, None, None, None),
        P(),
        P(),
        P(("scan", "row"), "col", None, None, None),
        P(("scan", "row"), "col"),
        P("scan"),
    )
    out_specs = P(("scan", "row"), "col", None, None, None, None)
    body = functools.partial(local, mesh.shape["row"], mesh.shape["col"])
    return jax.shard_map(body, mesh=mesh, in_specs=in_specs, out_specs=out_specs, check_vma=False)
```

time: 1040 us -> 376 us (0.36)
  the two profiles are of different devices: /device:TPU:64 before, /device:TPU:58 now
where the time goes in v1:
time: 376 us; the launch traced here: 374 us
  matrix products  119 us (32%)
  local copies, waits for them, and re-layouts  113 us (30%)
  Pallas kernels  92.9 us (25%)
  other arithmetic  25.7 us (7%)
  loops' own time  22.6 us (6%)
    pallas_call x1, Pallas kernels, fused(): pl.pallas_call(functools.partial(kernel, n_row, n_col), out_shape=(jax.Sh...  92.9 us
    cond x83, local copies, waits for them, and re-layouts  92.2 us
    sub x12, matrix products, one_head(): weights = jnp.where(mask[:, None, :], jnp.exp(masked - top), 0.0)  59.6 us
    dot_general x12, matrix products, one_head(): jnp.einsum('bqk,kd->bqd', probs, v, preferred_element_type=jnp.float32)  46.5 us
    another operation x1, loops' own time, local(): lax.cond(jnp.max(flag) > 0.0, lambda: stable(own, scale, w_qkv, blocks, r...  22.6 us
    and x18, other arithmetic, stable(): marks.append(valid[number] & inside & (pattern[block, 3 * dr + dc] > 0))  18.4 us
    dot_general x1, matrix products, dot(): lax.dot_general(a, b, (((1,), (0,)), ((), ())), preferred_element_type=jn...  12.4 us

profile of v1, /device:TPU:58, one launch (start us, length us, event | category | flops | bytes accessed | tf_op | source)
XLA Modules:
  0.0 373.6 jit_solution(12172074229593391508)
XLA Ops:
  2.0 92.9 %shard_map.78 = (bf16[512,768]{1,0:T(8,128)(2,1)}, f32[8,128]{1,0:T(8,128)S(1)}, bf16[12,128,768]{2,1,0:T(8,128)(2,1)}, bf16[16,16,768]{2,1,0:T(8,128)(2,1)}, s32[9,8,128]{2,1,0:T(8,128)}) custom-call(bf16[4,128,768]{2,1,0:T(8,128)(2,1)} %bitcast.143, f32[1,768]{1,0:T(1,128)S(1)} %reshape.138.gain_ref, bf16[768,2304]{1,0:T(8,128)(2,1)} %w_hbm.1, ...), custom_call_target="tpu_custom_call" | custom-call | flops 8254390272 | bytes 9437184 | tf_op jit(solution)/shard_map/pallas_call | solution.py:359
  96.2 275.3 %conditional.1 = (bf16[1,1,2,2,128,768]{5,4,3,2,1,0:T(8,128)(2,1)}) conditional(s32[]{:T(128)} %convert_element_type.18, bf16[512,768]{1,0:T(8,128)(2,1)} %get-tuple-element.79, (s32[9,8,128]{2,1,0:T(8,128)}, bf16[12,128,768]{2,1,0:T(8,128)(2,1)}, bf16[4,128,768]{2,1,0:T(8,128)(2,1)}, bf16[16,16,768]{2,1,0:T(8,128)(2,1)}, ...), branch_computations={%region_1.0_spmd, %region_2.9_spmd.clone} | conditional | flops 8489219584 | bytes 127142760 | solution.py:452
  113.9 12.4 %convolution_convert_fusion = bf16[2304,2304]{0,1:T(8,128)(2,1)S(1)} fusion(bf16[768,2304]{1,0:T(8,128)(2,1)} %get-tuple-element.94, bf16[2304,768]{1,0:T(8,128)(2,1)S(1)} %constant_dynamic-update-slice_fusion, f32[768]{0:T(1024)} %reduce, f32[2304]{0:T(1024)} %add_rsqrt_fusion, f32[2304]{0:T(1024)S(1)} %broadcast_multiply_fusion), kind=kOutput, calls=%fused_computation.28 | convolution fusion | flops 8167882752 | bytes 17716224 | tf_op jit(solution)/shard_map/cond/branch_1_fun/dot_general | solution.py:30
  127.7 2.6 copy-done.1
  131.2 1.5 gather_fusion
  132.7 5.4 %fusion.46 = (bf16[2304,768]{0,1:T(8,128)(2,1)S(1)}, bf16[2304,768]{0,1:T(8,128)(2,1)}) fusion(bf16[2304,2304]{0,1:T(8,128)(2,1)} %copy-done.1), kind=kLoop, calls=%fused_computation.119 | loop fusion | bytes 14155776 | tf_op jit(solution)/shard_map/cond/branch_1_fun/slice | solution.py:427
  174.3 1.4 dynamic-update-slice.40
  204.6 1.4 dynamic-update-slice.27
  206.0 1.4 dynamic-update-slice.28
  227.9 1.4 dynamic-update-slice.51
  230.7 1.4 dynamic-update-slice.53
  232.1 1.4 dynamic-update-slice.54
  233.5 1.4 dynamic-update-slice.55
  235.0 1.4 dynamic-update-slice.56
  236.4 1.4 dynamic-update-slice.57
  244.2 1.4 dynamic-update-slice.61
  249.8 1.4 dynamic-update-slice.65
  252.6 1.4 dynamic-update-slice.67
  254.0 1.4 dynamic-update-slice.68
  255.5 1.4 dynamic-update-slice.69
  256.9 1.4 dynamic-update-slice.70
  258.3 1.4 dynamic-update-slice.71
  262.4 106.1 %while.10 = (s32[]{:T(128)}, bf16[12,4,128,64]{2,3,0,1:T(8,128)(2,1)}, pred[4,2304]{1,0:T(4,128)(4,1)}, bf16[12,4,128,64]{2,3,0,1:T(8,128)(2,1)}, bf16[12,2304,6...) while((s32[]{:T(128)}, bf16[12,4,128,64]{2,3,0,1:T(8,128)(2,1)}, ...), condition=%wide.region_8.8_spmd, body=%wide.region_5.7_spmd.sunk | while | flops 310282496 | bytes 10182733 | solution.py:438
  262.4 5.0 %fusion.59 = (f32[4,128]{1,0:T(4,128)S(1)}, f32[4,128,2304]{2,1,0:T(8,128)}) fusion(pred[4,2304]{1,0:T(4,128)(4,1)} %get-tuple-element.277, bf16[12,2304,64]{1,2,0:T(8,128)(2,1)} %get-tuple-element.279, s32[]{:T(128)} %get-tuple-element.268, bf16[12,4,128,64]{2,3,0,1:T(8,128)(2,1)} %get-tuple-element.278), kind=kOutput, calls=%fused_computation.118.clone.1 | convolution fusion | flops 156895488 | bytes 5100544 | tf_op jit(solution)/shard_map/cond/branch_1_fun/while/body/eval_jaxpr/sub | solution.py:434
  267.4 3.9 %fusion.60 = bf16[12,4,128,64]{2,3,0,1:T(8,128)(2,1)} fusion(bf16[12,4,128,64]{2,3,0,1:T(8,128)(2,1)} %get-tuple-element.269, s32[]{:T(128)} %get-tuple-element.268, f32[4,128,2304]{2,1,0:T(8,128)} %get-tuple-element.259, f32[4,128]{1,0:T(4,128)S(1)} %get-tuple-element.260, bf16[12,2304,64]{1,2,0:T(8,128)(2,1)S(1)} %get-tuple-element.280), kind=kOutput, calls=%fused_computation.11.clone.1 | convolution fusion | flops 153387008 | bytes 5082112 | tf_op jit(solution)/shard_map/cond/branch_1_fun/while/body/eval_jaxpr/bqk,kd->bqd/dot_general | solution.py:436
  271.3 5.0 %fusion.59 = (f32[4,128]{1,0:T(4,128)S(1)}, f32[4,128,2304]{2,1,0:T(8,128)}) fusion(pred[4,2304]{1,0:T(4,128)(4,1)} %get-tuple-element.277, bf16[12,2304,64]{1,2,0:T(8,128)(2,1)} %get-tuple-element.279, s32[]{:T(128)} %get-tuple-element.268, bf16[12,4,128,64]{2,3,0,1:T(8,128)(2,1)} %get-tuple-element.278), kind=kOutput, calls=%fused_computation.118.clone.1 | convolution fusion | flops 156895488 | bytes 5100544 | tf_op jit(solution)/shard_map/cond/branch_1_fun/while/body/eval_jaxpr/sub | solution.py:434
  276.2 3.9 %fusion.60 = bf16[12,4,128,64]{2,3,0,1:T(8,128)(2,1)} fusion(bf16[12,4,128,64]{2,3,0,1:T(8,128)(2,1)} %get-tuple-element.269, s32[]{:T(128)} %get-tuple-element.268, f32[4,128,2304]{2,1,0:T(8,128)} %get-tuple-element.259, f32[4,128]{1,0:T(4,128)S(1)} %get-tuple-element.260, bf16[12,2304,64]{1,2,0:T(8,128)(2,1)S(1)} %get-tuple-element.280), kind=kOutput, calls=%fused_computation.11.clone.1 | convolution fusion | flops 153387008 | bytes 5082112 | tf_op jit(solution)/shard_map/cond/branch_1_fun/while/body/eval_jaxpr/bqk,kd->bqd/dot_general | solution.py:436
  280.1 5.0 %fusion.59 = (f32[4,128]{1,0:T(4,128)S(1)}, f32[4,128,2304]{2,1,0:T(8,128)}) fusion(pred[4,2304]{1,0:T(4,128)(4,1)} %get-tuple-element.277, bf16[12,2304,64]{1,2,0:T(8,128)(2,1)} %get-tuple-element.279, s32[]{:T(128)} %get-tuple-element.268, bf16[12,4,128,64]{2,3,0,1:T(8,128)(2,1)} %get-tuple-element.278), kind=kOutput, calls=%fused_computation.118.clone.1 | convolution fusion | flops 156895488 | bytes 5100544 | tf_op jit(solution)/shard_map/cond/branch_1_fun/while/body/eval_jaxpr/sub | solution.py:434
  285.1 3.9 %fusion.60 = bf16[12,4,128,64]{2,3,0,1:T(8,128)(2,1)} fusion(bf16[12,4,128,64]{2,3,0,1:T(8,128)(2,1)} %get-tuple-element.269, s32[]{:T(128)} %get-tuple-element.268, f32[4,128,2304]{2,1,0:T(8,128)} %get-tuple-element.259, f32[4,128]{1,0:T(4,128)S(1)} %get-tuple-element.260, bf16[12,2304,64]{1,2,0:T(8,128)(2,1)S(1)} %get-tuple-element.280), kind=kOutput, calls=%fused_computation.11.clone.1 | convolution fusion | flops 153387008 | bytes 5082112 | tf_op jit(solution)/shard_map/cond/branch_1_fun/while/body/eval_jaxpr/bqk,kd->bqd/dot_general | solution.py:436
  289.0 5.0 %fusion.59 = (f32[4,128]{1,0:T(4,128)S(1)}, f32[4,128,2304]{2,1,0:T(8,128)}) fusion(pred[4,2304]{1,0:T(4,128)(4,1)} %get-tuple-element.277, bf16[12,2304,64]{1,2,0:T(8,128)(2,1)} %get-tuple-element.279, s32[]{:T(128)} %get-tuple-element.268, bf16[12,4,128,64]{2,3,0,1:T(8,128)(2,1)} %get-tuple-element.278), kind=kOutput, calls=%fused_computation.118.clone.1 | convolution fusion | flops 156895488 | bytes 5100544 | tf_op jit(solution)/shard_map/cond/branch_1_fun/while/body/eval_jaxpr/sub | solution.py:434
  293.9 3.9 %fusion.60 = bf16[12,4,128,64]{2,3,0,1:T(8,128)(2,1)} fusion(bf16[12,4,128,64]{2,3,0,1:T(8,128)(2,1)} %get-tuple-element.269, s32[]{:T(128)} %get-tuple-element.268, f32[4,128,2304]{2,1,0:T(8,128)} %get-tuple-element.259, f32[4,128]{1,0:T(4,128)S(1)} %get-tuple-element.260, bf16[12,2304,64]{1,2,0:T(8,128)(2,1)S(1)} %get-tuple-element.280), kind=kOutput, calls=%fused_computation.11.clone.1 | convolution fusion | flops 153387008 | bytes 5082112 | tf_op jit(solution)/shard_map/cond/branch_1_fun/while/body/eval_jaxpr/bqk,kd->bqd/dot_general | solution.py:436
  297.8 5.0 %fusion.59 = (f32[4,128]{1,0:T(4,128)S(1)}, f32[4,128,2304]{2,1,0:T(8,128)}) fusion(pred[4,2304]{1,0:T(4,128)(4,1)} %get-tuple-element.277, bf16[12,2304,64]{1,2,0:T(8,128)(2,1)} %get-tuple-element.279, s32[]{:T(128)} %get-tuple-element.268, bf16[12,4,128,64]{2,3,0,1:T(8,128)(2,1)} %get-tuple-element.278), kind=kOutput, calls=%fused_computation.118.clone.1 | convolution fusion | flops 156895488 | bytes 5100544 | tf_op jit(solution)/shard_map/cond/branch_1_fun/while/body/eval_jaxpr/sub | solution.py:434
  302.8 3.9 %fusion.60 = bf16[12,4,128,64]{2,3,0,1:T(8,128)(2,1)} fusion(bf16[12,4,128,64]{2,3,0,1:T(8,128)(2,1)} %get-tuple-element.269, s32[]{:T(128)} %get-tuple-element.268, f32[4,128,2304]{2,1,0:T(8,128)} %get-tuple-element.259, f32[4,128]{1,0:T(4,128)S(1)} %get-tuple-element.260, bf16[12,2304,64]{1,2,0:T(8,128)(2,1)S(1)} %get-tuple-element.280), kind=kOutput, calls=%fused_computation.11.clone.1 | convolution fusion | flops 153387008 | bytes 5082112 | tf_op jit(solution)/shard_map/cond/branch_1_fun/while/body/eval_jaxpr/bqk,kd->bqd/dot_general | solution.py:436
  306.6 5.0 %fusion.59 = (f32[4,128]{1,0:T(4,128)S(1)}, f32[4,128,2304]{2,1,0:T(8,128)}) fusion(pred[4,2304]{1,0:T(4,128)(4,1)} %get-tuple-element.277, bf16[12,2304,64]{1,2,0:T(8,128)(2,1)} %get-tuple-element.279, s32[]{:T(128)} %get-tuple-element.268, bf16[12,4,128,64]{2,3,0,1:T(8,128)(2,1)} %get-tuple-element.278), kind=kOutput, calls=%fused_computation.118.clone.1 | convolution fusion | flops 156895488 | bytes 5100544 | tf_op jit(solution)/shard_map/cond/branch_1_fun/while/body/eval_jaxpr/sub | solution.py:434
  311.6 3.9 %fusion.60 = bf16[12,4,128,64]{2,3,0,1:T(8,128)(2,1)} fusion(bf16[12,4,128,64]{2,3,0,1:T(8,128)(2,1)} %get-tuple-element.269, s32[]{:T(128)} %get-tuple-element.268, f32[4,128,2304]{2,1,0:T(8,128)} %get-tuple-element.259, f32[4,128]{1,0:T(4,128)S(1)} %get-tuple-element.260, bf16[12,2304,64]{1,2,0:T(8,128)(2,1)S(1)} %get-tuple-element.280), kind=kOutput, calls=%fused_computation.11.clone.1 | convolution fusion | flops 153387008 | bytes 5082112 | tf_op jit(solution)/shard_map/cond/branch_1_fun/while/body/eval_jaxpr/bqk,kd->bqd/dot_general | solution.py:436
  315.5 5.0 %fusion.59 = (f32[4,128]{1,0:T(4,128)S(1)}, f32[4,128,2304]{2,1,0:T(8,128)}) fusion(pred[4,2304]{1,0:T(4,128)(4,1)} %get-tuple-element.277, bf16[12,2304,64]{1,2,0:T(8,128)(2,1)} %get-tuple-element.279, s32[]{:T(128)} %get-tuple-element.268, bf16[12,4,128,64]{2,3,0,1:T(8,128)(2,1)} %get-tuple-element.278), kind=kOutput, calls=%fused_computation.118.clone.1 | convolution fusion | flops 156895488 | bytes 5100544 | tf_op jit(solution)/shard_map/cond/branch_1_fun/while/body/eval_jaxpr/sub | solution.py:434
  320.4 3.9 %fusion.60 = bf16[12,4,128,64]{2,3,0,1:T(8,128)(2,1)} fusion(bf16[12,4,128,64]{2,3,0,1:T(8,128)(2,1)} %get-tuple-element.269, s32[]{:T(128)} %get-tuple-element.268, f32[4,128,2304]{2,1,0:T(8,128)} %get-tuple-element.259, f32[4,128]{1,0:T(4,128)S(1)} %get-tuple-element.260, bf16[12,2304,64]{1,2,0:T(8,128)(2,1)S(1)} %get-tuple-element.280), kind=kOutput, calls=%fused_computation.11.clone.1 | convolution fusion | flops 153387008 | bytes 5082112 | tf_op jit(solution)/shard_map/cond/branch_1_fun/while/body/eval_jaxpr/bqk,kd->bqd/dot_general | solution.py:436
  324.3 5.0 %fusion.59 = (f32[4,128]{1,0:T(4,128)S(1)}, f32[4,128,2304]{2,1,0:T(8,128)}) fusion(pred[4,2304]{1,0:T(4,128)(4,1)} %get-tuple-element.277, bf16[12,2304,64]{1,2,0:T(8,128)(2,1)} %get-tuple-element.279, s32[]{:T(128)} %get-tuple-element.268, bf16[12,4,128,64]{2,3,0,1:T(8,128)(2,1)} %get-tuple-element.278), kind=kOutput, calls=%fused_computation.118.clone.1 | convolution fusion | flops 156895488 | bytes 5100544 | tf_op jit(solution)/shard_map/cond/branch_1_fun/while/body/eval_jaxpr/sub | solution.py:434
  329.3 3.9 %fusion.60 = bf16[12,4,128,64]{2,3,0,1:T(8,128)(2,1)} fusion(bf16[12,4,128,64]{2,3,0,1:T(8,128)(2,1)} %get-tuple-element.269, s32[]{:T(128)} %get-tuple-element.268, f32[4,128,2304]{2,1,0:T(8,128)} %get-tuple-element.259, f32[4,128]{1,0:T(4,128)S(1)} %get-tuple-element.260, bf16[12,2304,64]{1,2,0:T(8,128)(2,1)S(1)} %get-tuple-element.280), kind=kOutput, calls=%fused_computation.11.clone.1 | convolution fusion | flops 153387008 | bytes 5082112 | tf_op jit(solution)/shard_map/cond/branch_1_fun/while/body/eval_jaxpr/bqk,kd->bqd/dot_general | solution.py:436
  333.2 5.0 %fusion.59 = (f32[4,128]{1,0:T(4,128)S(1)}, f32[4,128,2304]{2,1,0:T(8,128)}) fusion(pred[4,2304]{1,0:T(4,128)(4,1)} %get-tuple-element.277, bf16[12,2304,64]{1,2,0:T(8,128)(2,1)} %get-tuple-element.279, s32[]{:T(128)} %get-tuple-element.268, bf16[12,4,128,64]{2,3,0,1:T(8,128)(2,1)} %get-tuple-element.278), kind=kOutput, calls=%fused_computation.118.clone.1 | convolution fusion | flops 156895488 | bytes 5100544 | tf_op jit(solution)/shard_map/cond/branch_1_fun/while/body/eval_jaxpr/sub | solution.py:434
  338.1 3.9 %fusion.60 = bf16[12,4,128,64]{2,3,0,1:T(8,128)(2,1)} fusion(bf16[12,4,128,64]{2,3,0,1:T(8,128)(2,1)} %get-tuple-element.269, s32[]{:T(128)} %get-tuple-element.268, f32[4,128,2304]{2,1,0:T(8,128)} %get-tuple-element.259, f32[4,128]{1,0:T(4,128)S(1)} %get-tuple-element.260, bf16[12,2304,64]{1,2,0:T(8,128)(2,1)S(1)} %get-tuple-element.280), kind=kOutput, calls=%fused_computation.11.clone.1 | convolution fusion | flops 153387008 | bytes 5082112 | tf_op jit(solution)/shard_map/cond/branch_1_fun/while/body/eval_jaxpr/bqk,kd->bqd/dot_general | solution.py:436
  342.0 5.0 %fusion.59 = (f32[4,128]{1,0:T(4,128)S(1)}, f32[4,128,2304]{2,1,0:T(8,128)}) fusion(pred[4,2304]{1,0:T(4,128)(4,1)} %get-tuple-element.277, bf16[12,2304,64]{1,2,0:T(8,128)(2,1)} %get-tuple-element.279, s32[]{:T(128)} %get-tuple-element.268, bf16[12,4,128,64]{2,3,0,1:T(8,128)(2,1)} %get-tuple-element.278), kind=kOutput, calls=%fused_computation.118.clone.1 | convolution fusion | flops 156895488 | bytes 5100544 | tf_op jit(solution)/shard_map/cond/branch_1_fun/while/body/eval_jaxpr/sub | solution.py:434
  347.0 3.9 %fusion.60 = bf16[12,4,128,64]{2,3,0,1:T(8,128)(2,1)} fusion(bf16[12,4,128,64]{2,3,0,1:T(8,128)(2,1)} %get-tuple-element.269, s32[]{:T(128)} %get-tuple-element.268, f32[4,128,2304]{2,1,0:T(8,128)} %get-tuple-element.259, f32[4,128]{1,0:T(4,128)S(1)} %get-tuple-element.260, bf16[12,2304,64]{1,2,0:T(8,128)(2,1)S(1)} %get-tuple-element.280), kind=kOutput, calls=%fused_computation.11.clone.1 | convolution fusion | flops 153387008 | bytes 5082112 | tf_op jit(solution)/shard_map/cond/branch_1_fun/while/body/eval_jaxpr/bqk,kd->bqd/dot_general | solution.py:436
  350.8 5.0 %fusion.59 = (f32[4,128]{1,0:T(4,128)S(1)}, f32[4,128,2304]{2,1,0:T(8,128)}) fusion(pred[4,2304]{1,0:T(4,128)(4,1)} %get-tuple-element.277, bf16[12,2304,64]{1,2,0:T(8,128)(2,1)} %get-tuple-element.279, s32[]{:T(128)} %get-tuple-element.268, bf16[12,4,128,64]{2,3,0,1:T(8,128)(2,1)} %get-tuple-element.278), kind=kOutput, calls=%fused_computation.118.clone.1 | convolution fusion | flops 156895488 | bytes 5100544 | tf_op jit(solution)/shard_map/cond/branch_1_fun/while/body/eval_jaxpr/sub | solution.py:434
  355.8 3.9 %fusion.60 = bf16[12,4,128,64]{2,3,0,1:T(8,128)(2,1)} fusion(bf16[12,4,128,64]{2,3,0,1:T(8,128)(2,1)} %get-tuple-element.269, s32[]{:T(128)} %get-tuple-element.268, f32[4,128,2304]{2,1,0:T(8,128)} %get-tuple-element.259, f32[4,128]{1,0:T(4,128)S(1)} %get-tuple-element.260, bf16[12,2304,64]{1,2,0:T(8,128)(2,1)S(1)} %get-tuple-element.280), kind=kOutput, calls=%fused_computation.11.clone.1 | convolution fusion | flops 153387008 | bytes 5082112 | tf_op jit(solution)/shard_map/cond/branch_1_fun/while/body/eval_jaxpr/bqk,kd->bqd/dot_general | solution.py:436
  359.7 5.0 %fusion.59 = (f32[4,128]{1,0:T(4,128)S(1)}, f32[4,128,2304]{2,1,0:T(8,128)}) fusion(pred[4,2304]{1,0:T(4,128)(4,1)} %get-tuple-element.277, bf16[12,2304,64]{1,2,0:T(8,128)(2,1)} %get-tuple-element.279, s32[]{:T(128)} %get-tuple-element.268, bf16[12,4,128,64]{2,3,0,1:T(8,128)(2,1)} %get-tuple-element.278), kind=kOutput, calls=%fused_computation.118.clone.1 | convolution fusion | flops 156895488 | bytes 5100544 | tf_op jit(solution)/shard_map/cond/branch_1_fun/while/body/eval_jaxpr/sub | solution.py:434
  364.7 3.9 %fusion.60 = bf16[12,4,128,64]{2,3,0,1:T(8,128)(2,1)} fusion(bf16[12,4,128,64]{2,3,0,1:T(8,128)(2,1)} %get-tuple-element.269, s32[]{:T(128)} %get-tuple-element.268, f32[4,128,2304]{2,1,0:T(8,128)} %get-tuple-element.259, f32[4,128]{1,0:T(4,128)S(1)} %get-tuple-element.260, bf16[12,2304,64]{1,2,0:T(8,128)(2,1)S(1)} %get-tuple-element.280), kind=kOutput, calls=%fused_computation.11.clone.1 | convolution fusion | flops 153387008 | bytes 5082112 | tf_op jit(solution)/shard_map/cond/branch_1_fun/while/body/eval_jaxpr/bqk,kd->bqd/dot_general | solution.py:436
  371.5 2.1 copy.114
  (119 shorter events, 103.8 us)
Async XLA Ops:
  1.3 0.7 copy-start
  2.0 94.2 %copy-start.4 = (s32[1,1,2,2,9]{4,3,2,1,0:T(2,128)S(1)}, s32[1,1,2,2,9]{4,3,2,1,0:T(2,128)}, u32[]{:S(2)}) copy-start(s32[1,1,2,2,9]{4,3,2,1,0:T(2,128)} %param.14) | copy-start | bytes 436
  96.3 0.6 copy-start.5
  96.8 8.6 %copy-start.2 = (bf16[4,128,768]{2,1,0:T(8,128)(2,1)S(1)}, bf16[4,128,768]{2,1,0:T(8,128)(2,1)}, u32[]{:S(2)}) copy-start(bf16[4,128,768]{2,1,0:T(8,128)(2,1)} %get-tuple-element.91) | copy-start | bytes 2359300 | tf_op jit(solution)/shard_map/cond
  96.8 13.4 %copy-start.3 = (bf16[16,16,768]{2,1,0:T(8,128)(2,1)S(1)}, bf16[16,16,768]{2,1,0:T(8,128)(2,1)}, u32[]{:S(2)}) copy-start(bf16[16,16,768]{2,1,0:T(8,128)(2,1)} %get-tuple-element.92) | copy-start | bytes 1179652 | tf_op jit(solution)/shard_map/cond
  126.3 4.0 %copy-start.1 = (bf16[2304,2304]{0,1:T(8,128)(2,1)}, bf16[2304,2304]{0,1:T(8,128)(2,1)S(1)}, u32[]{:S(2)}) copy-start(bf16[2304,2304]{0,1:T(8,128)(2,1)S(1)} %convolution_convert_fusion) | copy-start | bytes 31850500 | tf_op jit(solution)/shard_map/cond
  130.3 0.8 copy-start.7
  148.2 6.6 %copy-start.6 = (pred[512]{0:T(512)(128)(4,1)}, pred[512]{0:T(512)(128)(4,1)S(1)}, u32[]{:S(2)}) copy-start(pred[512]{0:T(512)(128)(4,1)S(1)} %broadcast.82) | copy-start | bytes 1540 | tf_op jit(solution)/shard_map/cond

commit v2 on v1

--- a/solution.py
+++ b/solution.py
@@ -4,6 +4,7 @@
 import jax.numpy as jnp
 from jax import lax
 from jax.experimental import pallas as pl
+from jax.experimental.layout import Layout, with_layout_constraint
 from jax.experimental.pallas import tpu as pltpu
 from jax.sharding import PartitionSpec as P
 
@@ -223,21 +224,16 @@
     def halves(pair, other):
         return jnp.where(low_half, pair, other), jnp.where(low_half, other, pair)
 
-    def project(rows, key_at, marks, part, out):
-        n = rows
-
-        def body(j, _):
-            at = pl.multiple_of(part * WIDTH + j * 256, 128)
-            result = dot(normed[0:n, :], weights[:, pl.ds(at, 256)]).astype(jnp.bfloat16)
+    def project(n, key_at, marks, part, out):
+        for j in range(3):
+            at = part * WIDTH + j * 256
+            result = dot(normed[0:n, :], weights[:, at : at + 256]).astype(jnp.bfloat16)
             for t in range(2):
                 pair = result[:, t * 128 : t * 128 + 128]
+                to = j * 512 + t * 256
                 first_head, second_head = halves(pair, marks)
-                to = pl.multiple_of(j * 512 + t * 256, 128)
-                out[pl.ds(key_at, n), pl.ds(to, 128)] = first_head
-                out[pl.ds(key_at, n), pl.ds(pl.multiple_of(to + 128, 128), 128)] = second_head
-            return 0
-
-        lax.fori_loop(0, 3, body, 0)
+                out[key_at : key_at + n, to : to + 128] = first_head
+                out[key_at : key_at + n, to + 128 : to + 256] = second_head
 
     def keys_values(values, key_at, places):
         n = values.shape[0]
@@ -249,37 +245,60 @@
         project(n, key_at, marks, 1, ka)
         project(n, key_at, jnp.ones((n, AUG), jnp.bfloat16), 2, va)
 
-    def attend(blocks, key_at, n, initial=False):
-        def body(h, _):
-            at = pl.ds(pl.multiple_of(h * AUG, 128), AUG)
-            if len(blocks) == 4:
-                q = qa[:, at]
-            else:
-                q = jnp.concatenate([qa[pl.ds(b * BLK, BLK), at] for b in blocks], axis=0)
-            scores = dot_t(q, ka[pl.ds(key_at, n), at])
-            probs = jnp.exp2(scores * EXP_SCALE).astype(jnp.bfloat16)
-            result = dot(probs, va[pl.ds(key_at, n), at])
-            if initial:
-                oa[:, at] = result
-            else:
-                for s, b in enumerate(blocks):
-                    oa[pl.ds(b * BLK, BLK), at] += result[s * BLK : s * BLK + BLK]
+    def lanes(pair, half):
+        return pl.ds(pl.multiple_of(pair * (2 * AUG) + half * AUG, AUG), AUG)
+
+    def part_of(rows, keys, at):
+        def stacked(ref):
+            return jnp.concatenate([ref[begin : begin + n, at] for begin, n in keys], axis=0)
+
+        begin, n = rows
+        scores = dot_t(qa[begin : begin + n, at], stacked(ka))
+        probs = jnp.exp2(scores * EXP_SCALE).astype(jnp.bfloat16)
+        return dot(probs, stacked(va))
+
+    def attend_own(begin, end):
+        def body(pair, _):
+            for half in range(2):
+                at = lanes(pair, half)
+                oa[:, at] = part_of((0, OWN_KEYS), ((0, OWN_KEYS),), at)
             return 0
 
-        lax.fori_loop(0, HEADS, body, 0)
+        lax.fori_loop(begin, end, body, 0)
+
+    def attend_halo():
+        def body(pair, _):
+            for half in range(2):
+                at = lanes(pair, half)
+                for b in range(4):
+                    i, j = divmod(b, 2)
+                    groups = ((2 * i, 2), (4 + 2 * j, 2), (8 + b, 1))
+                    keys = tuple((OWN_KEYS + slot * BLK, n * BLK) for slot, n in groups)
+                    rows = slice(b * BLK, b * BLK + BLK)
+                    oa[rows, at] += part_of((b * BLK, BLK), keys, at)
+            return 0
+
+        lax.fori_loop(0, HEADS // 2, body, 0)
+
+    def attend_region():
+        def body(pair, bad):
+            one, two = (
+                oa[:, lanes(pair, half)] + part_of((0, OWN_KEYS), ((REGION_AT, REGION),), lanes(pair, half))
+                for half in range(2)
+            )
+            sums = pltpu.roll(jnp.where(low_half, two, one), HDIM, 1)
+            result = jnp.where(low_half, one, two) / sums
+            out_ref[:, pl.ds(pl.multiple_of(pair * AUG, AUG), AUG)] = result.astype(jnp.bfloat16)
+            fine = (sums >= LOW) & (sums <= HIGH)
+            return jnp.maximum(bad, jnp.max(jnp.where(fine, 0.0, 1.0), axis=0, keepdims=True))
+
+        bad = lax.fori_loop(0, HEADS // 2, body, jnp.zeros((1, AUG), jnp.float32))
+        flag_ref[0, 0] = jnp.max(bad)
 
     loads[1].wait()
     keys_values(tokens, 0, OWN)
     q_marks = jnp.concatenate([jnp.broadcast_to(query_marks(b), (BLK, AUG)) for b in range(4)], axis=0)
     project(OWN_KEYS, 0, q_marks.astype(jnp.bfloat16), 0, qa)
-
-    arrive1()
-    total = part1[0].astype(jnp.float32)
-    for k in range(1, n_row):
-        total = total + part1[k].astype(jnp.float32)
-    mine[...] = total.astype(jnp.bfloat16)
-    start2()
-    part2[col] = mine[...]
 
     halo_wait((0, 1, 2, 3))
     send_halo(both(up, left), halo.at[0], 9, {"col": col - 1})
@@ -287,31 +306,34 @@
     send_halo(both(down, left), halo.at[2], 11, {"col": col - 1})
     send_halo(both(down, right), halo.at[3], 10, {"col": col + 1})
 
-    attend((0, 1, 2, 3), 0, OWN_KEYS, initial=True)
+    def merge(slots, number):
+        total = slots[0].astype(jnp.float32)
+        for k in range(1, number):
+            total = total + slots[k].astype(jnp.float32)
+        return total.astype(jnp.bfloat16)
+
+    arrive1()
+    mine[...] = merge(part1, n_row)
+    start2()
+    part2[col] = mine[...]
+
+    attend_own(0, 3)
 
     arrive2()
-    total = part2[0].astype(jnp.float32)
-    for k in range(1, n_col):
-        total = total + part2[k].astype(jnp.float32)
-    rtok[row] = total.astype(jnp.bfloat16)
+    rtok[row] = merge(part2, n_col)
     start3()
+
+    attend_own(3, 6)
 
     for exists, _, arrives in cnt_copies:
         pl.when(exists)(lambda arrives=arrives: arrives.wait_recv())
-
-    for group, blocks in enumerate(((0, 1), (2, 3), (0, 2), (1, 3))):
-        slots = (2 * group, 2 * group + 1)
-        if group >= 2:
-            halo_wait(slots)
-        key_at = OWN_KEYS + 2 * group * BLK
-        keys_values(halo[2 * group : 2 * group + 2].reshape(2 * BLK, WIDTH), key_at, [SLOTS[s] for s in slots])
-        attend(blocks, key_at, 2 * BLK)
+    halo_wait((4, 5, 6, 7))
+    keys_values(halo[0:8].reshape(8 * BLK, WIDTH), OWN_KEYS, SLOTS[0:8])
+    halo_wait((8, 9, 10, 11))
+    keys_values(halo[8:12].reshape(4 * BLK, WIDTH), OWN_KEYS + 8 * BLK, SLOTS[8:12])
+    attend_halo()
 
     arrive3()
-    keys_values(rtok[...].reshape(REGION, WIDTH), REGION_AT, None)
-    attend((0, 1, 2, 3), REGION_AT, REGION)
-
-    halo_wait((8, 9, 10, 11))
     saves = [
         pltpu.make_async_copy(halo, halo_out, save_sem.at[0]),
         pltpu.make_async_copy(rtok, rtok_out, save_sem.at[1]),
@@ -319,23 +341,8 @@
     ]
     for save in saves:
         save.start()
-    keys_values(halo[8:12].reshape(4 * BLK, WIDTH), OWN_KEYS + 8 * BLK, SLOTS[8:12])
-    for b in range(4):
-        attend((b,), OWN_KEYS + (8 + b) * BLK, BLK)
-
-    valid = lax.broadcasted_iota(jnp.int32, (OWN_KEYS, AUG), 0) < count
-
-    def finish(p, bad):
-        one = oa[:, pl.ds(pl.multiple_of(p * 256, 128), 128)]
-        two = oa[:, pl.ds(pl.multiple_of(p * 256 + 128, 128), 128)]
-        sums = pltpu.roll(jnp.where(low_half, two, one), HDIM, 1)
-        result = jnp.where(low_half, one, two) / sums
-        out_ref[:, pl.ds(pl.multiple_of(p * 128, 128), 128)] = jnp.where(valid, result, 0.0).astype(jnp.bfloat16)
-        fine = (sums >= LOW) & (sums <= HIGH)
-        return jnp.maximum(bad, jnp.max(jnp.where(fine, 0.0, 1.0), axis=0, keepdims=True))
-
-    bad = lax.fori_loop(0, 6, finish, jnp.zeros((1, AUG), jnp.float32))
-    flag_ref[...] = jnp.broadcast_to(bad, (8, AUG))
+    keys_values(rtok[...].reshape(REGION, WIDTH), REGION_AT, None)
+    attend_region()
 
     for cond, copy in sends:
         pl.when(cond)(lambda copy=copy: copy.wait_send())
@@ -360,13 +367,13 @@
         functools.partial(kernel, n_row, n_col),
         out_shape=(
             jax.ShapeDtypeStruct((OWN_KEYS, WIDTH), bf16),
-            jax.ShapeDtypeStruct((8, AUG), f32),
+            jax.ShapeDtypeStruct((1, 1), f32),
             jax.ShapeDtypeStruct((len(SLOTS), BLK, WIDTH), bf16),
             jax.ShapeDtypeStruct((n_row, chunk, WIDTH), bf16),
             jax.ShapeDtypeStruct((9, 8, 128), jnp.int32),
         ),
         in_specs=[anywhere, vmem, anywhere, smem, smem, vmem],
-        out_specs=(vmem, vmem, anywhere, anywhere, anywhere),
+        out_specs=(vmem, smem, anywhere, anywhere, anywhere),
         scratch_shapes=[
             pltpu.VMEM((4, BLK, WIDTH), bf16),
             pltpu.VMEM((len(SLOTS), BLK, WIDTH), bf16),
@@ -377,7 +384,7 @@
             pltpu.VMEM((chunk, WIDTH), bf16),
             pltpu.VMEM((n_col, chunk, WIDTH), bf16),
             pltpu.VMEM((n_row, chunk, WIDTH), bf16),
-            pltpu.VMEM((OWN_KEYS, WIDTH), bf16),
+            pltpu.VMEM((8 * BLK, WIDTH), bf16),
             pltpu.VMEM((OWN_KEYS, HEADS * AUG), bf16),
             pltpu.VMEM((KEYS, HEADS * AUG), bf16),
             pltpu.VMEM((KEYS, HEADS * AUG), bf16),
@@ -437,8 +444,7 @@
 
     heads = lax.map(one_head, (query.transpose(2, 0, 1, 3), key.transpose(1, 0, 2), value.transpose(1, 0, 2)))
     joined = heads.transpose(1, 2, 0, 3).reshape(OWN_KEYS, WIDTH)
-    live = jnp.arange(OWN_KEYS) < cnts[4, 0, 0]
-    return jnp.where(live[:, None], joined, jnp.zeros_like(joined))
+    return with_layout_constraint(joined, Layout(major_to_minor=(0, 1)))
 
 
 def local(n_row, n_col, tokens, gain, w_qkv, pattern, counts, region):
@@ -450,11 +456,12 @@
     )
     row, col = lax.axis_index("row"), lax.axis_index("col")
     result = lax.cond(
-        jnp.max(flag) > 0.0,
+        flag[0, 0] > 0.0,
         lambda: stable(own, scale, w_qkv, blocks, row, col, n_row, n_col, halo, rtok, cnts),
         lambda: out,
     )
-    return result.reshape(tokens.shape)
+    live = jnp.arange(OWN_KEYS, dtype=jnp.int32) < counts[0, 0]
+    return jnp.where(live[:, None], result, jnp.zeros_like(result)).reshape(tokens.shape)
 
 
 def solution(mesh):

time: 376 us -> 350 us (0.931)
  the two profiles are of different devices: /device:TPU:58 before, /device:TPU:8 now
where the time goes in v2:
time: 350 us; the launch traced here: 347 us
  matrix products  119 us (34%)
  local copies, waits for them, and re-layouts  113 us (32%)
  Pallas kernels  65.9 us (19%)
  other arithmetic  25.7 us (7%)
  loops' own time  22.9 us (7%)
    cond x81, local copies, waits for them, and re-layouts  91.4 us
    pallas_call x1, Pallas kernels, fused(): pl.pallas_call(functools.partial(kernel, n_row, n_col), out_shape=(jax.Sh...  65.9 us
    sub x12, matrix products, one_head(): weights = jnp.where(mask[:, None, :], jnp.exp(masked - top), 0.0)  59.6 us
    dot_general x12, matrix products, one_head(): jnp.einsum('bqk,kd->bqd', probs, v, preferred_element_type=jnp.float32)  46.5 us
    another operation x1, loops' own time, local(): lax.cond(flag[0, 0] > 0.0, lambda: stable(own, scale, w_qkv, blocks, row,...  22.9 us
    and x18, other arithmetic, stable(): marks.append(valid[number] & inside & (pattern[block, 3 * dr + dc] > 0))  18.5 us
    dot_general x1, matrix products, dot(): lax.dot_general(a, b, (((1,), (0,)), ((), ())), preferred_element_type=jn...  12.4 us

profile of v2, /device:TPU:8, one launch (start us, length us, event | category | flops | bytes accessed | tf_op | source)
XLA Modules:
  0.0 346.9 jit_solution(13788471177754026334)
XLA Ops:
  2.0 65.9 %shard_map.75 = (bf16[512,768]{1,0:T(8,128)(2,1)}, f32[1,1]{1,0:T(1,128)}, bf16[12,128,768]{2,1,0:T(8,128)(2,1)}, bf16[16,16,768]{2,1,0:T(8,128)(2,1)}, s32[9,8,128]{2,1,0:T(8,128)}) custom-call(bf16[4,128,768]{2,1,0:T(8,128)(2,1)} %bitcast.151, f32[1,768]{1,0:T(1,128)S(1)} %reshape.126.gain_ref, bf16[768,2304]{1,0:T(8,128)(2,1)} %w_hbm.1, ...), custom_call_target="tpu_custom_call" | custom-call | flops 8254390272 | bytes 9437184 | tf_op jit(solution)/shard_map/pallas_call | solution.py:366
  68.6 276.2 %conditional.1 = (bf16[512,768]{1,0:T(8,128)(2,1)}) conditional(s32[]{:T(128)} %bitcast.10, bf16[512,768]{1,0:T(8,128)(2,1)} %get-tuple-element.77, (bf16[12,128,768]{2,1,0:T(8,128)(2,1)}, bf16[4,128,768]{2,1,0:T(8,128)(2,1)}, bf16[16,16,768]{2,1,0:T(8,128)(2,1)}, f32[1,768]{1,0:T(1,128)}, bf16[768,2304]{1,0:T(8,128)(2,1)}, ...), branch_computations={%region_0.0_spmd, %region_1.8_spmd.clone} | conditional | flops 8488823808 | bytes 128702288 | solution.py:458
  85.8 12.4 %convolution_convert_fusion = bf16[2304,2304]{0,1:T(8,128)(2,1)S(1)} fusion(bf16[768,2304]{1,0:T(8,128)(2,1)} %get-tuple-element.91, bf16[2304,768]{1,0:T(8,128)(2,1)S(1)} %constant_dynamic-update-slice_fusion, f32[768]{0:T(1024)} %reduce, f32[2304]{0:T(1024)} %add_rsqrt_fusion, f32[2304]{0:T(1024)S(1)} %broadcast_multiply_fusion), kind=kOutput, calls=%fused_computation.28 | convolution fusion | flops 8167882752 | bytes 17716224 | tf_op jit(solution)/shard_map/cond/branch_1_fun/dot_general | solution.py:31
  99.7 2.6 copy-done.1
  103.2 1.5 gather_fusion
  104.7 5.4 %fusion.46 = (bf16[2304,768]{0,1:T(8,128)(2,1)S(1)}, bf16[2304,768]{0,1:T(8,128)(2,1)}) fusion(bf16[2304,2304]{0,1:T(8,128)(2,1)} %copy-done.1), kind=kLoop, calls=%fused_computation.120 | loop fusion | bytes 14155776 | tf_op jit(solution)/shard_map/cond/branch_1_fun/slice | solution.py:434
  189.2 1.4 dynamic-update-slice.46
  193.2 1.4 dynamic-update-slice.47
  199.2 1.4 dynamic-update-slice.50
  200.7 1.4 dynamic-update-slice.51
  205.0 1.4 dynamic-update-slice.54
  206.4 1.4 dynamic-update-slice.55
  207.8 1.4 dynamic-update-slice.56
  209.3 1.4 dynamic-update-slice.57
  220.0 1.4 dynamic-update-slice.63
  221.5 1.4 dynamic-update-slice.64
  222.9 1.4 dynamic-update-slice.65
  225.8 1.4 dynamic-update-slice.67
  227.2 1.4 dynamic-update-slice.68
  228.6 1.4 dynamic-update-slice.69
  231.5 1.4 dynamic-update-slice.71
  235.6 106.1 %while.10 = (s32[]{:T(128)}, bf16[12,4,128,64]{2,3,1,0:T(8,128)(2,1)}, pred[4,2304]{1,0:T(4,128)(4,1)}, bf16[12,4,128,64]{2,3,0,1:T(8,128)(2,1)}, bf16[12,2304,6...) while((s32[]{:T(128)}, bf16[12,4,128,64]{2,3,1,0:T(8,128)(2,1)}, ...), condition=%wide.region_7.7_spmd, body=%wide.region_4.6_spmd.sunk | while | flops 310282496 | bytes 10182733 | solution.py:445
  235.6 5.0 %fusion.59 = (f32[4,128]{1,0:T(4,128)S(1)}, f32[4,128,2304]{2,1,0:T(8,128)}) fusion(pred[4,2304]{1,0:T(4,128)(4,1)} %get-tuple-element.266, bf16[12,2304,64]{1,2,0:T(8,128)(2,1)} %get-tuple-element.268, s32[]{:T(128)} %get-tuple-element.257, bf16[12,4,128,64]{2,3,0,1:T(8,128)(2,1)} %get-tuple-element.267), kind=kOutput, calls=%fused_computation.119.clone.1 | convolution fusion | flops 156895488 | bytes 5100544 | tf_op jit(solution)/shard_map/cond/branch_1_fun/while/body/eval_jaxpr/sub | solution.py:441
  240.6 3.9 %fusion.60 = bf16[12,4,128,64]{2,3,1,0:T(8,128)(2,1)} fusion(bf16[12,4,128,64]{2,3,1,0:T(8,128)(2,1)} %get-tuple-element.258, s32[]{:T(128)} %get-tuple-element.257, f32[4,128,2304]{2,1,0:T(8,128)} %get-tuple-element.248, f32[4,128]{1,0:T(4,128)S(1)} %get-tuple-element.249, bf16[12,2304,64]{1,2,0:T(8,128)(2,1)S(1)} %get-tuple-element.269), kind=kOutput, calls=%fused_computation.11.clone.1 | convolution fusion | flops 153387008 | bytes 5082112 | tf_op jit(solution)/shard_map/cond/branch_1_fun/while/body/eval_jaxpr/bqk,kd->bqd/dot_general | solution.py:443
  244.4 5.0 %fusion.59 = (f32[4,128]{1,0:T(4,128)S(1)}, f32[4,128,2304]{2,1,0:T(8,128)}) fusion(pred[4,2304]{1,0:T(4,128)(4,1)} %get-tuple-element.266, bf16[12,2304,64]{1,2,0:T(8,128)(2,1)} %get-tuple-element.268, s32[]{:T(128)} %get-tuple-element.257, bf16[12,4,128,64]{2,3,0,1:T(8,128)(2,1)} %get-tuple-element.267), kind=kOutput, calls=%fused_computation.119.clone.1 | convolution fusion | flops 156895488 | bytes 5100544 | tf_op jit(solution)/shard_map/cond/branch_1_fun/while/body/eval_jaxpr/sub | solution.py:441
  249.4 3.9 %fusion.60 = bf16[12,4,128,64]{2,3,1,0:T(8,128)(2,1)} fusion(bf16[12,4,128,64]{2,3,1,0:T(8,128)(2,1)} %get-tuple-element.258, s32[]{:T(128)} %get-tuple-element.257, f32[4,128,2304]{2,1,0:T(8,128)} %get-tuple-element.248, f32[4,128]{1,0:T(4,128)S(1)} %get-tuple-element.249, bf16[12,2304,64]{1,2,0:T(8,128)(2,1)S(1)} %get-tuple-element.269), kind=kOutput, calls=%fused_computation.11.clone.1 | convolution fusion | flops 153387008 | bytes 5082112 | tf_op jit(solution)/shard_map/cond/branch_1_fun/while/body/eval_jaxpr/bqk,kd->bqd/dot_general | solution.py:443
  253.3 5.0 %fusion.59 = (f32[4,128]{1,0:T(4,128)S(1)}, f32[4,128,2304]{2,1,0:T(8,128)}) fusion(pred[4,2304]{1,0:T(4,128)(4,1)} %get-tuple-element.266, bf16[12,2304,64]{1,2,0:T(8,128)(2,1)} %get-tuple-element.268, s32[]{:T(128)} %get-tuple-element.257, bf16[12,4,128,64]{2,3,0,1:T(8,128)(2,1)} %get-tuple-element.267), kind=kOutput, calls=%fused_computation.119.clone.1 | convolution fusion | flops 156895488 | bytes 5100544 | tf_op jit(solution)/shard_map/cond/branch_1_fun/while/body/eval_jaxpr/sub | solution.py:441
  258.2 3.9 %fusion.60 = bf16[12,4,128,64]{2,3,1,0:T(8,128)(2,1)} fusion(bf16[12,4,128,64]{2,3,1,0:T(8,128)(2,1)} %get-tuple-element.258, s32[]{:T(128)} %get-tuple-element.257, f32[4,128,2304]{2,1,0:T(8,128)} %get-tuple-element.248, f32[4,128]{1,0:T(4,128)S(1)} %get-tuple-element.249, bf16[12,2304,64]{1,2,0:T(8,128)(2,1)S(1)} %get-tuple-element.269), kind=kOutput, calls=%fused_computation.11.clone.1 | convolution fusion | flops 153387008 | bytes 5082112 | tf_op jit(solution)/shard_map/cond/branch_1_fun/while/body/eval_jaxpr/bqk,kd->bqd/dot_general | solution.py:443
  262.1 5.0 %fusion.59 = (f32[4,128]{1,0:T(4,128)S(1)}, f32[4,128,2304]{2,1,0:T(8,128)}) fusion(pred[4,2304]{1,0:T(4,128)(4,1)} %get-tuple-element.266, bf16[12,2304,64]{1,2,0:T(8,128)(2,1)} %get-tuple-element.268, s32[]{:T(128)} %get-tuple-element.257, bf16[12,4,128,64]{2,3,0,1:T(8,128)(2,1)} %get-tuple-element.267), kind=kOutput, calls=%fused_computation.119.clone.1 | convolution fusion | flops 156895488 | bytes 5100544 | tf_op jit(solution)/shard_map/cond/branch_1_fun/while/body/eval_jaxpr/sub | solution.py:441
  267.1 3.9 %fusion.60 = bf16[12,4,128,64]{2,3,1,0:T(8,128)(2,1)} fusion(bf16[12,4,128,64]{2,3,1,0:T(8,128)(2,1)} %get-tuple-element.258, s32[]{:T(128)} %get-tuple-element.257, f32[4,128,2304]{2,1,0:T(8,128)} %get-tuple-element.248, f32[4,128]{1,0:T(4,128)S(1)} %get-tuple-element.249, bf16[12,2304,64]{1,2,0:T(8,128)(2,1)S(1)} %get-tuple-element.269), kind=kOutput, calls=%fused_computation.11.clone.1 | convolution fusion | flops 153387008 | bytes 5082112 | tf_op jit(solution)/shard_map/cond/branch_1_fun/while/body/eval_jaxpr/bqk,kd->bqd/dot_general | solution.py:443
  271.0 5.0 %fusion.59 = (f32[4,128]{1,0:T(4,128)S(1)}, f32[4,128,2304]{2,1,0:T(8,128)}) fusion(pred[4,2304]{1,0:T(4,128)(4,1)} %get-tuple-element.266, bf16[12,2304,64]{1,2,0:T(8,128)(2,1)} %get-tuple-element.268, s32[]{:T(128)} %get-tuple-element.257, bf16[12,4,128,64]{2,3,0,1:T(8,128)(2,1)} %get-tuple-element.267), kind=kOutput, calls=%fused_computation.119.clone.1 | convolution fusion | flops 156895488 | bytes 5100544 | tf_op jit(solution)/shard_map/cond/branch_1_fun/while/body/eval_jaxpr/sub | solution.py:441
  275.9 3.9 %fusion.60 = bf16[12,4,128,64]{2,3,1,0:T(8,128)(2,1)} fusion(bf16[12,4,128,64]{2,3,1,0:T(8,128)(2,1)} %get-tuple-element.258, s32[]{:T(128)} %get-tuple-element.257, f32[4,128,2304]{2,1,0:T(8,128)} %get-tuple-element.248, f32[4,128]{1,0:T(4,128)S(1)} %get-tuple-element.249, bf16[12,2304,64]{1,2,0:T(8,128)(2,1)S(1)} %get-tuple-element.269), kind=kOutput, calls=%fused_computation.11.clone.1 | convolution fusion | flops 153387008 | bytes 5082112 | tf_op jit(solution)/shard_map/cond/branch_1_fun/while/body/eval_jaxpr/bqk,kd->bqd/dot_general | solution.py:443
  279.8 5.0 %fusion.59 = (f32[4,128]{1,0:T(4,128)S(1)}, f32[4,128,2304]{2,1,0:T(8,128)}) fusion(pred[4,2304]{1,0:T(4,128)(4,1)} %get-tuple-element.266, bf16[12,2304,64]{1,2,0:T(8,128)(2,1)} %get-tuple-element.268, s32[]{:T(128)} %get-tuple-element.257, bf16[12,4,128,64]{2,3,0,1:T(8,128)(2,1)} %get-tuple-element.267), kind=kOutput, calls=%fused_computation.119.clone.1 | convolution fusion | flops 156895488 | bytes 5100544 | tf_op jit(solution)/shard_map/cond/branch_1_fun/while/body/eval_jaxpr/sub | solution.py:441
  284.8 3.9 %fusion.60 = bf16[12,4,128,64]{2,3,1,0:T(8,128)(2,1)} fusion(bf16[12,4,128,64]{2,3,1,0:T(8,128)(2,1)} %get-tuple-element.258, s32[]{:T(128)} %get-tuple-element.257, f32[4,128,2304]{2,1,0:T(8,128)} %get-tuple-element.248, f32[4,128]{1,0:T(4,128)S(1)} %get-tuple-element.249, bf16[12,2304,64]{1,2,0:T(8,128)(2,1)S(1)} %get-tuple-element.269), kind=kOutput, calls=%fused_computation.11.clone.1 | convolution fusion | flops 153387008 | bytes 5082112 | tf_op jit(solution)/shard_map/cond/branch_1_fun/while/body/eval_jaxpr/bqk,kd->bqd/dot_general | solution.py:443
  288.6 5.0 %fusion.59 = (f32[4,128]{1,0:T(4,128)S(1)}, f32[4,128,2304]{2,1,0:T(8,128)}) fusion(pred[4,2304]{1,0:T(4,128)(4,1)} %get-tuple-element.266, bf16[12,2304,64]{1,2,0:T(8,128)(2,1)} %get-tuple-element.268, s32[]{:T(128)} %get-tuple-element.257, bf16[12,4,128,64]{2,3,0,1:T(8,128)(2,1)} %get-tuple-element.267), kind=kOutput, calls=%fused_computation.119.clone.1 | convolution fusion | flops 156895488 | bytes 5100544 | tf_op jit(solution)/shard_map/cond/branch_1_fun/while/body/eval_jaxpr/sub | solution.py:441
  293.6 3.9 %fusion.60 = bf16[12,4,128,64]{2,3,1,0:T(8,128)(2,1)} fusion(bf16[12,4,128,64]{2,3,1,0:T(8,128)(2,1)} %get-tuple-element.258, s32[]{:T(128)} %get-tuple-element.257, f32[4,128,2304]{2,1,0:T(8,128)} %get-tuple-element.248, f32[4,128]{1,0:T(4,128)S(1)} %get-tuple-element.249, bf16[12,2304,64]{1,2,0:T(8,128)(2,1)S(1)} %get-tuple-element.269), kind=kOutput, calls=%fused_computation.11.clone.1 | convolution fusion | flops 153387008 | bytes 5082112 | tf_op jit(solution)/shard_map/cond/branch_1_fun/while/body/eval_jaxpr/bqk,kd->bqd/dot_general | solution.py:443
  297.5 5.0 %fusion.59 = (f32[4,128]{1,0:T(4,128)S(1)}, f32[4,128,2304]{2,1,0:T(8,128)}) fusion(pred[4,2304]{1,0:T(4,128)(4,1)} %get-tuple-element.266, bf16[12,2304,64]{1,2,0:T(8,128)(2,1)} %get-tuple-element.268, s32[]{:T(128)} %get-tuple-element.257, bf16[12,4,128,64]{2,3,0,1:T(8,128)(2,1)} %get-tuple-element.267), kind=kOutput, calls=%fused_computation.119.clone.1 | convolution fusion | flops 156895488 | bytes 5100544 | tf_op jit(solution)/shard_map/cond/branch_1_fun/while/body/eval_jaxpr/sub | solution.py:441
  302.4 3.9 %fusion.60 = bf16[12,4,128,64]{2,3,1,0:T(8,128)(2,1)} fusion(bf16[12,4,128,64]{2,3,1,0:T(8,128)(2,1)} %get-tuple-element.258, s32[]{:T(128)} %get-tuple-element.257, f32[4,128,2304]{2,1,0:T(8,128)} %get-tuple-element.248, f32[4,128]{1,0:T(4,128)S(1)} %get-tuple-element.249, bf16[12,2304,64]{1,2,0:T(8,128)(2,1)S(1)} %get-tuple-element.269), kind=kOutput, calls=%fused_computation.11.clone.1 | convolution fusion | flops 153387008 | bytes 5082112 | tf_op jit(solution)/shard_map/cond/branch_1_fun/while/body/eval_jaxpr/bqk,kd->bqd/dot_general | solution.py:443
  306.3 5.0 %fusion.59 = (f32[4,128]{1,0:T(4,128)S(1)}, f32[4,128,2304]{2,1,0:T(8,128)}) fusion(pred[4,2304]{1,0:T(4,128)(4,1)} %get-tuple-element.266, bf16[12,2304,64]{1,2,0:T(8,128)(2,1)} %get-tuple-element.268, s32[]{:T(128)} %get-tuple-element.257, bf16[12,4,128,64]{2,3,0,1:T(8,128)(2,1)} %get-tuple-element.267), kind=kOutput, calls=%fused_computation.119.clone.1 | convolution fusion | flops 156895488 | bytes 5100544 | tf_op jit(solution)/shard_map/cond/branch_1_fun/while/body/eval_jaxpr/sub | solution.py:441
  311.3 3.9 %fusion.60 = bf16[12,4,128,64]{2,3,1,0:T(8,128)(2,1)} fusion(bf16[12,4,128,64]{2,3,1,0:T(8,128)(2,1)} %get-tuple-element.258, s32[]{:T(128)} %get-tuple-element.257, f32[4,128,2304]{2,1,0:T(8,128)} %get-tuple-element.248, f32[4,128]{1,0:T(4,128)S(1)} %get-tuple-element.249, bf16[12,2304,64]{1,2,0:T(8,128)(2,1)S(1)} %get-tuple-element.269), kind=kOutput, calls=%fused_computation.11.clone.1 | convolution fusion | flops 153387008 | bytes 5082112 | tf_op jit(solution)/shard_map/cond/branch_1_fun/while/body/eval_jaxpr/bqk,kd->bqd/dot_general | solution.py:443
  315.2 5.0 %fusion.59 = (f32[4,128]{1,0:T(4,128)S(1)}, f32[4,128,2304]{2,1,0:T(8,128)}) fusion(pred[4,2304]{1,0:T(4,128)(4,1)} %get-tuple-element.266, bf16[12,2304,64]{1,2,0:T(8,128)(2,1)} %get-tuple-element.268, s32[]{:T(128)} %get-tuple-element.257, bf16[12,4,128,64]{2,3,0,1:T(8,128)(2,1)} %get-tuple-element.267), kind=kOutput, calls=%fused_computation.119.clone.1 | convolution fusion | flops 156895488 | bytes 5100544 | tf_op jit(solution)/shard_map/cond/branch_1_fun/while/body/eval_jaxpr/sub | solution.py:441
  320.1 3.9 %fusion.60 = bf16[12,4,128,64]{2,3,1,0:T(8,128)(2,1)} fusion(bf16[12,4,128,64]{2,3,1,0:T(8,128)(2,1)} %get-tuple-element.258, s32[]{:T(128)} %get-tuple-element.257, f32[4,128,2304]{2,1,0:T(8,128)} %get-tuple-element.248, f32[4,128]{1,0:T(4,128)S(1)} %get-tuple-element.249, bf16[12,2304,64]{1,2,0:T(8,128)(2,1)S(1)} %get-tuple-element.269), kind=kOutput, calls=%fused_computation.11.clone.1 | convolution fusion | flops 153387008 | bytes 5082112 | tf_op jit(solution)/shard_map/cond/branch_1_fun/while/body/eval_jaxpr/bqk,kd->bqd/dot_general | solution.py:443
  324.0 5.0 %fusion.59 = (f32[4,128]{1,0:T(4,128)S(1)}, f32[4,128,2304]{2,1,0:T(8,128)}) fusion(pred[4,2304]{1,0:T(4,128)(4,1)} %get-tuple-element.266, bf16[12,2304,64]{1,2,0:T(8,128)(2,1)} %get-tuple-element.268, s32[]{:T(128)} %get-tuple-element.257, bf16[12,4,128,64]{2,3,0,1:T(8,128)(2,1)} %get-tuple-element.267), kind=kOutput, calls=%fused_computation.119.clone.1 | convolution fusion | flops 156895488 | bytes 5100544 | tf_op jit(solution)/shard_map/cond/branch_1_fun/while/body/eval_jaxpr/sub | solution.py:441
  329.0 3.9 %fusion.60 = bf16[12,4,128,64]{2,3,1,0:T(8,128)(2,1)} fusion(bf16[12,4,128,64]{2,3,1,0:T(8,128)(2,1)} %get-tuple-element.258, s32[]{:T(128)} %get-tuple-element.257, f32[4,128,2304]{2,1,0:T(8,128)} %get-tuple-element.248, f32[4,128]{1,0:T(4,128)S(1)} %get-tuple-element.249, bf16[12,2304,64]{1,2,0:T(8,128)(2,1)S(1)} %get-tuple-element.269), kind=kOutput, calls=%fused_computation.11.clone.1 | convolution fusion | flops 153387008 | bytes 5082112 | tf_op jit(solution)/shard_map/cond/branch_1_fun/while/body/eval_jaxpr/bqk,kd->bqd/dot_general | solution.py:443
  332.8 5.0 %fusion.59 = (f32[4,128]{1,0:T(4,128)S(1)}, f32[4,128,2304]{2,1,0:T(8,128)}) fusion(pred[4,2304]{1,0:T(4,128)(4,1)} %get-tuple-element.266, bf16[12,2304,64]{1,2,0:T(8,128)(2,1)} %get-tuple-element.268, s32[]{:T(128)} %get-tuple-element.257, bf16[12,4,128,64]{2,3,0,1:T(8,128)(2,1)} %get-tuple-element.267), kind=kOutput, calls=%fused_computation.119.clone.1 | convolution fusion | flops 156895488 | bytes 5100544 | tf_op jit(solution)/shard_map/cond/branch_1_fun/while/body/eval_jaxpr/sub | solution.py:441
  337.8 3.9 %fusion.60 = bf16[12,4,128,64]{2,3,1,0:T(8,128)(2,1)} fusion(bf16[12,4,128,64]{2,3,1,0:T(8,128)(2,1)} %get-tuple-element.258, s32[]{:T(128)} %get-tuple-element.257, f32[4,128,2304]{2,1,0:T(8,128)} %get-tuple-element.248, f32[4,128]{1,0:T(4,128)S(1)} %get-tuple-element.249, bf16[12,2304,64]{1,2,0:T(8,128)(2,1)S(1)} %get-tuple-element.269), kind=kOutput, calls=%fused_computation.11.clone.1 | convolution fusion | flops 153387008 | bytes 5082112 | tf_op jit(solution)/shard_map/cond/branch_1_fun/while/body/eval_jaxpr/bqk,kd->bqd/dot_general | solution.py:443
  341.7 1.8 copy.13
  344.8 2.1 broadcast_select_fusion
  (119 shorter events, 103.3 us)
Async XLA Ops:
  0.7 67.2 %copy-start.5 = (f32[1,768]{1,0:T(1,128)}, f32[1,768]{1,0:T(1,128)S(1)}, u32[]{:S(2)}) copy-start(f32[1,768]{1,0:T(1,128)S(1)} %reshape.126.gain_ref) | copy-start | bytes 9220
  1.3 0.7 copy-start
  2.0 66.5 %copy-start.4 = (s32[1,1,2,2,9]{4,3,2,1,0:T(2,128)S(1)}, s32[1,1,2,2,9]{4,3,2,1,0:T(2,128)}, u32[]{:S(2)}) copy-start(s32[1,1,2,2,9]{4,3,2,1,0:T(2,128)} %param.14) | copy-start | bytes 436
  68.8 8.6 %copy-start.2 = (bf16[4,128,768]{2,1,0:T(8,128)(2,1)S(1)}, bf16[4,128,768]{2,1,0:T(8,128)(2,1)}, u32[]{:S(2)}) copy-start(bf16[4,128,768]{2,1,0:T(8,128)(2,1)} %get-tuple-element.88) | copy-start | bytes 2359300 | tf_op jit(solution)/shard_map/cond
  68.8 13.4 %copy-start.3 = (bf16[16,16,768]{2,1,0:T(8,128)(2,1)S(1)}, bf16[16,16,768]{2,1,0:T(8,128)(2,1)}, u32[]{:S(2)}) copy-start(bf16[16,16,768]{2,1,0:T(8,128)(2,1)} %get-tuple-element.89) | copy-start | bytes 1179652 | tf_op jit(solution)/shard_map/cond
  98.3 4.0 %copy-start.1 = (bf16[2304,2304]{0,1:T(8,128)(2,1)}, bf16[2304,2304]{0,1:T(8,128)(2,1)S(1)}, u32[]{:S(2)}) copy-start(bf16[2304,2304]{0,1:T(8,128)(2,1)S(1)} %convolution_convert_fusion) | copy-start | bytes 31850500 | tf_op jit(solution)/shard_map/cond
  102.3 0.8 copy-start.7
  120.5 6.8 %copy-start.6 = (pred[512]{0:T(512)(128)(4,1)}, pred[512]{0:T(512)(128)(4,1)S(1)}, u32[]{:S(2)}) copy-start(pred[512]{0:T(512)(128)(4,1)S(1)} %broadcast.63) | copy-start | bytes 1540 | tf_op jit(solution)/shard_map/cond
